TPU v7x, 128 devices: a whole 4x4x4 slice. The times are simulated.
128 devices in a mesh: seq: 16 (over x, y), section: 8 (over z, core).
Axes of the slice: x: 4, y: 4, z: 4, core: 2. Of those that a mesh axis runs over, the one named last changes fastest.
Arguments:
- hidden: bfloat16 [8, 6144, 2560], P('section', 'seq'), may hold values from -6 to 6
- query_norm_gain: float32 [8, 2560], P('section'), may hold values from 0.25 to 1.75
- key_norm_gain: float32 [8, 2560], P('section'), may hold values from 0.25 to 1.75
- text_kv: bfloat16 [8, 16, 2, 512, 2560], P('section', 'seq'), may hold values from -6 to 6
- holder: int32 [8], P('section'), may hold values from 0 to 15
- pattern: int32 [48, 7], replicated, may hold values from 0 to 1, as said below
- grad_out: bfloat16 [8, 6144, 2560], P('section', 'seq'), may hold values from -6 to 6
Outputs:
- attended: bfloat16 [8, 6144, 2560], P('section', 'seq')
- upstream: bfloat16 [8, 6144, 2560], P('section', 'seq')
- text_grad: bfloat16 [8, 2, 512, 2560], P('section')
Inputs may be any that keep to these rules, and one draw needn't show every extreme that they name: pattern[b, 3] = 1 for every block b; entries are 0 or 1.
All inputs are finite; a program needn't handle non-finite values.
Results may differ from a plain program's by a relative error of at most 0.0078.
Values may be sent and summed in bfloat16 or wider, within the bound.
A program may use at most 256 MiB of HBM per device.

v0:
```python
import jax
import jax.numpy as jnp
from jax import lax
from jax.sharding import PartitionSpec as P

HDIM = 128
BLK = 128


eps = 1e-06


def extended(cells, sides, width):
    for axis, dim in sides:
        count = lax.axis_size(axis)
        ends = count - 1
        head = lax.slice_in_dim(cells, 0, width, axis=dim)
        tail = lax.slice_in_dim(cells, cells.shape[dim] - width, cells.shape[dim], axis=dim)
        cells = jnp.concatenate(
            [
                lax.ppermute(tail, axis, [(i, (i + 1) % count) for i in range(ends)]),
                cells,
                lax.ppermute(head, axis, [((i + 1) % count, i) for i in range(ends)]),
            ],
            axis=dim,
        )
    return cells


def from_root(block, axis, owner):
    block = jnp.where(lax.axis_index(axis) == owner, block, jnp.zeros_like(block))
    return lax.psum(block, axis)


def shifted(x, axis, by):
    peers = lax.axis_size(axis)
    pairs = [(i, i + by) for i in range(peers) if 0 <= i + by < peers]
    return lax.ppermute(x, axis, pairs)


def norm_forward(hidden_state, norm_gain):
    hidden_float = hidden_state.astype(jnp.float32)
    inverse_root_norm = lax.rsqrt(
        jnp.mean(hidden_float * hidden_float, axis=-1, keepdims=True) + eps
    )
    normalized_input = hidden_float * inverse_root_norm
    return (
        (normalized_input * norm_gain).astype(jnp.bfloat16),
        normalized_input,
        inverse_root_norm,
    )


def norm_backward(upper_bound, norm_gain, normalized_input, inverse_root_norm):
    scaled_input = upper_bound * norm_gain
    return inverse_root_norm * (
        scaled_input
        - normalized_input * jnp.mean(scaled_input * normalized_input, axis=-1, keepdims=True)
    )


def block_mask(pattern, slab, bpd, nslab):
    span = pattern.shape[1]
    rows = lax.dynamic_slice_in_dim(pattern, slab * bpd, bpd, 0)
    first = jnp.arange(bpd, dtype=jnp.int32)[:, None]
    second = jnp.arange(3 * bpd, dtype=jnp.int32)[None, :]
    offset = second - first
    onehot = offset[:, :, None] == jnp.arange(span, dtype=jnp.int32)[None, None, :]
    picked = jnp.sum(jnp.where(onehot, rows[:, None, :], 0), axis=-1)
    globe = slab * bpd - bpd + second
    inside = (globe >= 0) & (globe < nslab * bpd)
    return (picked > 0) & inside


def token_mask(blocks):
    return jnp.repeat(jnp.repeat(blocks, BLK, axis=0), BLK, axis=1)


def divide_heads(x):
    return x.reshape(x.shape[0], x.shape[1] // HDIM, HDIM).transpose(1, 0, 2)


def join_heads(x):
    return x.transpose(1, 0, 2).reshape(x.shape[1], x.shape[0] * x.shape[2])


def query_side(qh, kh, vh, tkh, tvh, doh, attend_mask):
    scale = qh.shape[-1] ** (-0.5)
    keys = jnp.concatenate([kh, tkh], axis=0)
    vals = jnp.concatenate([vh, tvh], axis=0)
    full = jnp.concatenate([attend_mask, jnp.ones((qh.shape[0], tkh.shape[0]), bool)], axis=1)
    scores = jnp.dot(qh, keys.T, preferred_element_type=jnp.float32) * scale
    scores = jnp.where(full, scores, -1e30)
    top = jnp.max(scores, axis=1, keepdims=True)
    total = jnp.sum(jnp.where(full, jnp.exp(scores - top), 0.0), axis=1, keepdims=True)
    lse = top + jnp.log(total)
    probs = jnp.where(full, jnp.exp(scores - lse), 0.0)
    probs_b = probs.astype(jnp.bfloat16)
    out = jnp.dot(probs_b, vals, preferred_element_type=jnp.float32)
    dprob = jnp.dot(doh, vals.T, preferred_element_type=jnp.float32)
    delta = jnp.sum(doh.astype(jnp.float32) * out, axis=1)
    dscore = (probs * (dprob - delta[:, None]) * scale).astype(jnp.bfloat16)
    query_gradient = jnp.dot(dscore, keys, preferred_element_type=jnp.float32)
    dkeys = jnp.dot(dscore.T, qh, preferred_element_type=jnp.float32)
    dvals = jnp.dot(probs_b.T, doh, preferred_element_type=jnp.float32)
    return (out, lse[:, 0], delta, query_gradient, dkeys, dvals)


def local(hidden, query_norm_gain, key_norm_gain, text_kv, holder, pattern, grad_out):
    hidden_state = hidden[0]
    output_gradient = grad_out[0]
    token_rows = hidden_state.shape[0]
    bpd = token_rows // BLK
    slab = lax.axis_index("seq")
    nslab = lax.axis_size("seq")
    normed_query, normalized_input, inverse_root_norm = norm_forward(
        hidden_state, query_norm_gain[0]
    )
    kn, _, _ = norm_forward(hidden_state, key_norm_gain[0])
    near = extended(jnp.stack([kn, hidden_state]), (("seq", 1),), token_rows)
    text_tokens = from_root(text_kv[0, 0], "seq", holder[0])
    attend_mask = token_mask(block_mask(pattern, slab, bpd, nslab))

    def each_head_value(a):
        return query_side(a[0], a[1], a[2], a[3], a[4], a[5], attend_mask)

    saved_residuals = lax.map(
        each_head_value,
        (
            divide_heads(normed_query),
            divide_heads(near[0]),
            divide_heads(near[1]),
            divide_heads(text_tokens[0]),
            divide_heads(text_tokens[1]),
            divide_heads(output_gradient),
        ),
    )
    out, lse, delta, query_gradient, dkeys, dvals = saved_residuals
    ext_rows = 3 * token_rows
    dtext_part = jnp.stack([join_heads(dkeys[:, ext_rows:]), join_heads(dvals[:, ext_rows:])])
    ext = jnp.stack([join_heads(dkeys[:, :ext_rows]), join_heads(dvals[:, :ext_rows])])
    from_upper = shifted(ext[:, :token_rows].astype(jnp.bfloat16), "seq", -1).astype(jnp.float32)
    from_lower = shifted(ext[:, 2 * token_rows :].astype(jnp.bfloat16), "seq", 1).astype(
        jnp.float32
    )
    own_rows = ext[:, token_rows : 2 * token_rows] + from_upper + from_lower
    text_total = lax.psum(dtext_part, "seq")
    grad_hidden = (
        own_rows[1]
        + norm_backward(
            join_heads(query_gradient), query_norm_gain[0], normalized_input, inverse_root_norm
        )
        + norm_backward(own_rows[0], key_norm_gain[0], normalized_input, inverse_root_norm)
    )
    upstream = shifted(grad_hidden.astype(jnp.bfloat16), "section", -1)
    attended = join_heads(out).astype(jnp.bfloat16)
    return (attended[None], upstream[None], text_total.astype(jnp.bfloat16)[None])


def solution(mesh):
    in_specs = (
        P("section", "seq", None),
        P("section", None),
        P("section", None),
        P("section", "seq", None, None, None),
        P("section"),
        P(),
        P("section", "seq", None),
    )
    out_specs = (
        P("section", "seq", None),
        P("section", "seq", None),
        P("section", None, None, None),
    )
    return jax.shard_map(local, mesh=mesh, in_specs=in_specs, out_specs=out_specs, check_vma=False)
```

profile of v0, /device:TPU:1, one launch (start us, length us, event | category | flops | bytes accessed | tf_op | source)
XLA Modules:
  0.0 922.6 jit_solution(16334344849139469414)
XLA Ops:
  7.2 2.8 copy.43
  16.0 6.6 collective-permute-start
  23.3 8.0 copy.45
  31.3 2.7 select_bitcast_fusion
  34.7 4.0 copy.46
  38.7 3.2 fusion.42
  41.9 89.1 %collective-permute-done.1 = bf16[2,384,2560]{1,2,0:T(8,128)(2,1)} collective-permute-done((bf16[2,384,2560]{1,2,0:T(8,128)(2,1)}, bf16[2,384,2560]{1,2,0:T(8,128)(2,1)}, u32[]{:S(2)}, u32[]{:S(2)}) %collective-permute-start.1) | collective-permute-done | bytes 3932192 | tf_op jit(solution)/shard_map/ppermute | solution.py:23
  131.1 2.8 collective-permute-done
  133.9 5.2 pad_maximum_fusion.7
  139.1 4.9 fusion.45
  143.9 32.0 %all-reduce.4.cloned.1.call-done = bf16[2,512,2560]{1,2,0:T(8,128)(2,1)} async-done(((bf16[2,512,2560]{1,2,0:T(8,128)(2,1)}), bf16[2,512,2560]{1,2,0:T(8,128)(2,1)}) %all-reduce.4.cloned.1.call-update) | async-done | bytes 5242896 | tf_op jit(solution)/shard_map/psum | solution.py:32
  175.9 5.2 fusion.46
  181.1 351.3 %while.17 = (s32[]{:T(128)}, bf16[20,384,128]{1,2,0:T(8,128)(2,1)}, f32[20,384,128]{1,2,0:T(8,128)}, f32[20,1664,128]{1,2,0:T(8,128)}, f32[20,1664,128]{1,2,0:T(...) while((s32[]{:T(128)}, bf16[20,384,128]{1,2,0:T(8,128)(2,1)}, ...), condition=%wide.region_7.8_spmd.clone, body=%wide.region_3.7_spmd.clone.sunk | while | flops 996523264 | bytes 28792892 | solution.py:127
  351.8 2.6 fusion.70
  369.4 2.6 fusion.70
  457.3 2.6 fusion.70
  532.4 9.7 %slice.46 = f32[20,1152,128]{1,2,0:T(8,128)} slice(f32[20,1664,128]{1,2,0:T(8,128)} %get-tuple-element.70), slice={[0:20], [0:1152], [0:128]} | slice | bytes 23592960 | tf_op jit(solution)/shard_map/slice | solution.py:141
  542.2 9.7 %slice.45 = f32[20,1152,128]{1,2,0:T(8,128)} slice(f32[20,1664,128]{1,2,0:T(8,128)} %get-tuple-element.69), slice={[0:20], [0:1152], [0:128]} | slice | bytes 23592960 | tf_op jit(solution)/shard_map/slice | solution.py:141
  551.9 9.0 fusion.29
  560.9 3.6 fusion.44
  565.8 5.9 collective-permute-start.3
  571.7 5.7 slice.53
  577.3 5.6 slice.52
  583.0 10.1 %pad_maximum_fusion.8 = f32[2,512,2560]{1,2,0:T(8,128)} fusion(f32[1,512,2560]{1,2,0:T(8,128)} %bitcast.170, f32[1,512,2560]{1,2,0:T(8,128)} %bitcast.171), kind=kLoop, calls=%fused_computation.47 | loop fusion | flops 2621440 | bytes 20971520 | tf_op jit(solution)/shard_map/stack | solution.py:140
  593.1 3.9 fusion.40
  597.0 55.5 %collective-permute-done.2 = bf16[2,384,2560]{1,2,0:T(8,128)(2,1)} collective-permute-done((bf16[2,384,2560]{1,2,0:T(8,128)(2,1)}, bf16[2,384,2560]{1,2,0:T(8,128)(2,1)}, u32[]{:S(2)}, u32[]{:S(2)}) %collective-permute-start.2) | collective-permute-done | bytes 3932192 | tf_op jit(solution)/shard_map/ppermute | solution.py:38
  653.4 5.0 fusion.32
  660.5 3.0 fusion.36
  663.6 3.9 collective-permute-start.4
  667.4 234.0 %all-reduce.5 = bf16[2,512,2560]{1,2,0:T(8,128)(2,1)} all-reduce(f32[2,512,2560]{1,2,0:T(8,128)} %pad_maximum_fusion.8), channel_id=1, replica_groups=mesh['seq'=16,'section'=8] {'seq'}, use_global_device_ids=true, to_apply=%region_10.11 | all-reduce | flops 2621440 | bytes 15728640 | tf_op jit(solution)/shard_map/psum | solution.py:147
  903.9 7.9 copy.62
  911.8 4.0 copy.61
  (430 shorter events, 355.8 us)
Async XLA Ops:
  7.2 26.9 %copy-start = (s32[48,7]{0,1:T(8,128)S(1)}, s32[48,7]{0,1:T(8,128)}, u32[]{:S(2)}) copy-start(s32[48,7]{0,1:T(8,128)} %param.14) | copy-start | bytes 4036
  7.2 168.7 %all-reduce.4.cloned.1.call-start = ((), (), s32[]{:S(2)}) async-start(), calls=%async_computation | async-start | bytes 10485760 | tf_op jit(solution)/shard_map/psum | solution.py:32
  14.7 116.3 %collective-permute-start.1 = (bf16[2,384,2560]{1,2,0:T(8,128)(2,1)}, bf16[2,384,2560]{1,2,0:T(8,128)(2,1)}, u32[]{:S(2)}, u32[]{:S(2)}) collective-permute-start(bf16[2,384,2560]{1,2,0:T(8,128)(2,1)} %pad_maximum_fusion.9), channel_id=1, source_target_pairs={{8,0},{16,8},{24,16},{32,24},{40,32},{48,40},{56,48},{64,56},{72,6... | collective-permute-start | bytes 11796488 | tf_op jit(solution)/shard_map/ppermute | solution.py:23
  16.0 117.9 %collective-permute-start = (bf16[2,384,2560]{1,2,0:T(8,128)(2,1)}, bf16[2,384,2560]{1,2,0:T(8,128)(2,1)}, u32[]{:S(2)}, u32[]{:S(2)}) collective-permute-start(bf16[2,384,2560]{1,2,0:T(8,128)(2,1)} %pad_maximum_fusion.9), channel_id=1, source_target_pairs={{0,8},{8,16},{16,24},{24,32},{32,40},{40,48},{48,56},{56,64},{64,7... | collective-permute-start | bytes 11796488 | tf_op jit(solution)/shard_map/ppermute | solution.py:21
  38.7 95.2 %copy-start.3 = (bf16[1,384,2560]{1,2,0:T(8,128)(2,1)S(1)}, bf16[1,384,2560]{1,2,0:T(8,128)(2,1)}, u32[]{:S(2)}) copy-start(bf16[1,384,2560]{1,2,0:T(8,128)(2,1)} %copy-done.2) | copy-start | bytes 5898244
  186.8 3.9 copy-start.5
  204.4 3.9 copy-start.5
  222.0 3.9 copy-start.5
  239.5 3.9 copy-start.5
  257.0 3.9 copy-start.5
  274.6 3.9 copy-start.5
  292.1 3.9 copy-start.5
  309.7 3.9 copy-start.5
  327.2 3.9 copy-start.5
  344.7 3.9 copy-start.5
  362.4 3.9 copy-start.5
  380.1 3.9 copy-start.5
  397.6 3.9 copy-start.5
  415.2 3.9 copy-start.5
  432.7 3.9 copy-start.5
  450.2 3.9 copy-start.5
  467.9 3.9 copy-start.5
  485.5 3.9 copy-start.5
  520.6 3.9 copy-start.5
  564.5 88.0 %collective-permute-start.2 = (bf16[2,384,2560]{1,2,0:T(8,128)(2,1)}, bf16[2,384,2560]{1,2,0:T(8,128)(2,1)}, u32[]{:S(2)}, u32[]{:S(2)}) collective-permute-start(bf16[2,384,2560]{1,2,0:T(8,128)(2,1)} %get-tuple-element.175), channel_id=1, source_target_pairs={{8,0},{16,8},{24,16},{32,24},{40,32},{48,40},{56,48},{64,56},{72,6... | collective-permute-start | bytes 11796488 | tf_op jit(solution)/shard_map/ppermute | solution.py:38
  565.8 87.6 %collective-permute-start.3 = (bf16[2,384,2560]{1,2,0:T(8,128)(2,1)}, bf16[2,384,2560]{1,2,0:T(8,128)(2,1)}, u32[]{:S(2)}, u32[]{:S(2)}) collective-permute-start(bf16[2,384,2560]{1,2,0:T(8,128)(2,1)} %get-tuple-element.176), channel_id=1, source_target_pairs={{0,8},{8,16},{16,24},{24,32},{32,40},{40,48},{48,56},{56,64},{64,7... | collective-permute-start | bytes 11796488 | tf_op jit(solution)/shard_map/ppermute | solution.py:38
  583.0 70.5 %slice-start = ((s8[11796480]{0:T(1024)(128)(4,1)}), s8[4194304]{0:T(1024)(128)(4,1)S(1)}, s32[]{:S(2)}) async-start(s8[11796480]{0:T(1024)(128)(4,1)} %bitcast.162), calls=%async_computation.1 | async-start | bytes 8388608
  583.0 70.5 %slice-start.1 = ((s8[11796480]{0:T(1024)(128)(4,1)}), s8[4194304]{0:T(1024)(128)(4,1)S(1)}, s32[]{:S(2)}) async-start(s8[11796480]{0:T(1024)(128)(4,1)} %bitcast.162), calls=%async_computation.2 | async-start | bytes 8388608
  583.0 70.5 %slice-start.2 = ((s8[11796480]{0:T(1024)(128)(4,1)}), s8[3407872]{0:T(1024)(128)(4,1)S(1)}, s32[]{:S(2)}) async-start(s8[11796480]{0:T(1024)(128)(4,1)} %bitcast.162), calls=%async_computation.3 | async-start | bytes 6815744
  663.5 237.9 %copy-start.6 = (bf16[20,384,128]{1,2,0:T(8,128)(2,1)S(1)}, bf16[20,384,128]{1,2,0:T(8,128)(2,1)}, u32[]{:S(2)}) copy-start(bf16[20,384,128]{1,2,0:T(8,128)(2,1)} %get-tuple-element.68) | copy-start | bytes 5898244
  663.6 248.2 %collective-permute-start.4 = (bf16[384,2560]{0,1:T(8,128)(2,1)}, bf16[384,2560]{0,1:T(8,128)(2,1)}, u32[]{:S(2)}, u32[]{:S(2)}) collective-permute-start(bf16[384,2560]{0,1:T(8,128)(2,1)} %fusion.36), channel_id=1, source_target_pairs={{1,0},{2,1},{3,2},{4,3},{5,4},{6,5},{7,6},{9,8},{10,9},{11,10},{12... | collective-permute-start | bytes 5898248 | tf_op jit(solution)/shard_map/ppermute | solution.py:38
  903.9 11.9 %copy-start.1 = (s32[48,7]{0,1:T(8,128)S(1)}, s32[48,7]{0,1:T(8,128)}, u32[]{:S(2)}) copy-start(s32[48,7]{0,1:T(8,128)} %param.14) | copy-start | bytes 4036
  (5 other events, 11.4 us)
Sparse Core Ops, SparseCore 0:
  34.1 141.7 all-reduce.3
where the time goes:
time: 929 us; the launch traced here: 923 us
  matrix products  237 us (26%)
  blocking collectives  234 us (25%)
  waiting for transfers between devices  180 us (19%)
  local copies, waits for them, and re-layouts  158 us (17%)
  other arithmetic  79 us (9%)
  starting transfers between devices  19 us (2%)
  between operations  14.9 us (2%)
    psum x1, blocking collectives, local(): text_total = lax.psum(dtext_part, 'seq')  234 us
    ppermute x1, waiting for transfers between devices, extended(): lax.ppermute(head, axis, [((i + 1) % count, i) for i in range(ends)])  89.1 us
    dynamic_slice x120, local copies, waits for them, and re-layouts, local(): lax.map(each_head_value, (divide_heads(normed_query), divide_heads(near[0...  68.1 us
    ppermute x3, waiting for transfers between devices, shifted(): return lax.ppermute(x, axis, pairs)  56.4 us
    dot_general x20, matrix products, query_side(): dvals = jnp.dot(probs_b.T, doh, preferred_element_type=jnp.float32)  51.2 us
    dot_general x20, matrix products, query_side(): out = jnp.dot(probs_b, vals, preferred_element_type=jnp.float32)  46 us
    dot_general x20, matrix products, query_side(): dkeys = jnp.dot(dscore.T, qh, preferred_element_type=jnp.float32)  44.5 us
    dot_general x20, matrix products, query_side(): dprob = jnp.dot(doh, vals.T, preferred_element_type=jnp.float32)  38.1 us
  transfers between devices with their start and end apart: 6, of which 5 were waited for; matrix products, arithmetic and copies ran while one was open for 7% of the time, Pallas kernels for 0%

commit v1 on v0

v1 whole, which is shorter than its diff:
```python
import jax
import jax.numpy as jnp
from jax import lax
from jax.experimental import pallas as pl
from jax.experimental.pallas import tpu as pltpu
from jax.sharding import PartitionSpec as P

HDIM = 128
BLK = 128
EPS = 1e-06
MESH = pl.DeviceIdType.MESH

NX = 4
NY = 4
SLAB = 384
TXT = 512
WIDTH = 2560
STEPS = 5
OWN = NY * SLAB
EXT = OWN + 2 * SLAB
KEYS = EXT + TXT
QT = 256
KC = 256
NCHUNK = 4 + TXT // KC
SCALE = HDIM ** (-0.5)
LOG2E = 1.4426950408889634
NEG = -1e30

(
    K_H,
    K_DO,
    K_TX,
    K_TY,
    K_TG,
    K_HALO,
    K_ATT,
    K_AH,
    K_A,
    K_RS,
    K_G1,
    K_G2,
) = range(12)
KINDS = 12
O_R, O_RH, O_MH, O_M = range(4)

f32 = jnp.float32
bf16 = jnp.bfloat16


def dot_nn(a, b):
    return lax.dot_general(a, b, (((1,), (0,)), ((), ())), preferred_element_type=f32)


def dot_nt(a, b):
    return lax.dot_general(a, b, (((1,), (1,)), ((), ())), preferred_element_type=f32)


def block(k):
    return pl.ds(pl.multiple_of(k * BLK, BLK), BLK)


def span(start, size, unit):
    return pl.ds(pl.multiple_of(start, unit), size)


def packed(column):
    rows = column.shape[0]
    wide = jnp.broadcast_to(column, (rows, BLK))
    return [wide[b * BLK : (b + 1) * BLK].T[:8] for b in range(rows // BLK)]


def unpacked(tile):
    return jnp.broadcast_to(tile[:1], (BLK, BLK)).T


def kernel(
    hid, do_in, txt, gq_ref, gk_ref, sel_ref, qb_ref,
    att_out, dh_out, tg_out,
    HS, HX, DO, RTX, RT, RB, T1, TS, T2, T3, KA, KT, VT, QA, S, PB, DK, DV, DQ,
    ATT, AFS, AH, AHR, AO, AF, M, MH, MT, MHS, MHR, MR, TGP, TG1, TG2, TGY, TGX, DH,
    send, recv, once_send, once_recv, loc, loc1,
):
    seq = lax.axis_index("seq")
    x = lax.div(seq, NY)
    y = lax.rem(seq, NY)

    def ry(d):
        return lax.rem(y + (d + NY), NY)

    def rx(d):
        return lax.rem(x + (d + NX), NX)

    def yid(d):
        return {"seq": x * NY + ry(d)}

    def xid(d):
        return {"seq": rx(d) * NY + y}

    def rc(src, dst, kind, j, d, dev):
        return pltpu.make_async_remote_copy(
            src_ref=src, dst_ref=dst, send_sem=send.at[kind, j, d],
            recv_sem=recv.at[kind, j, d], device_id=dev, device_id_type=MESH,
        )

    def rc1(src, dst, kind, d, dev):
        return pltpu.make_async_remote_copy(
            src_ref=src, dst_ref=dst, send_sem=once_send.at[kind, d],
            recv_sem=once_recv.at[kind, d], device_id=dev, device_id_type=MESH,
        )

    def hcol(j, yy):
        return block(NY * j + yy)

    def wide(j):
        return span(j * (NY * BLK), NY * BLK, NY * BLK)

    def slab(yy):
        return span(SLAB + SLAB * yy, SLAB, SLAB)

    def oslab(yy):
        return span(SLAB * yy, SLAB, SLAB)

    def cp_h(j, d, w=False):
        return rc(hid.at[:, hcol(j, ry(d))], HX.at[j, slab(ry(-d) if w else y), :], K_H, j, d, yid(d))

    def cp_do(j, d, w=False):
        return rc(do_in.at[:, hcol(j, ry(d))], DO.at[j, oslab(ry(-d) if w else y), :], K_DO, j, d, yid(d))

    def cp_tx(j, d, w=False):
        return rc(txt.at[:, block(rx(d)), wide(j)], T1.at[j, rx(-d) if w else x], K_TX, j, d, xid(d))

    def cp_ty(j, d, w=False):
        return rc(TS.at[j, :, :, block(ry(d))], T2.at[j, ry(-d) if w else y], K_TY, j, d, yid(d))

    def cp_tg(j, d, w=False):
        return rc(T3.at[j, :, block(x), :], T3.at[j, :, block(rx(-d) if w else x), :], K_TG, j, d, xid(d))

    def cp_halo(j, d, w=False):
        if d == 1:
            return rc(HX.at[j, pl.ds(OWN, SLAB), :], HX.at[j, pl.ds(0, SLAB), :], K_HALO, j, 1, xid(1))
        return rc(HX.at[j, pl.ds(SLAB, SLAB), :], HX.at[j, pl.ds(OWN + SLAB, SLAB), :], K_HALO, j, 3, xid(3))

    def cp_att(j, d, w=False):
        return rc(ATT.at[j, oslab(ry(d)), :], att_out.at[:, hcol(j, ry(-d) if w else y)], K_ATT, j, d, yid(d))

    def cp_ah(j, d, w=False):
        k = 1 if d == 1 else 0
        return rc(AH.at[j, k], AHR.at[j, 1 - k], K_AH, j, d, xid(d))

    def cp_a(j, d, w=False):
        return rc(AO.at[j, oslab(ry(d)), :], AF.at[:, hcol(j, ry(-d) if w else y)], K_A, j, d, yid(d))

    def cp_rs(j, d, w=False):
        return rc(TGP.at[j, :, block(rx(d)), :], TG1.at[j, rx(-d) if w else x], K_RS, j, d, xid(d))

    def cp_g1k(j, d, w=False):
        return rc(TG2.at[j, 0], TGY.at[j, :, block(ry(-d) if w else y)], K_G1, j, d, yid(d))

    def cp_g1v(j, d, w=False):
        return rc(TG2.at[j, 1], TGX.at[j, block(rx(-d) if w else x), :], K_G1, j, 4 + d, xid(d))

    def cp_g2k(j, d, w=False):
        return rc(TGY.at[j], tg_out.at[0, block(rx(-d) if w else x), wide(j)], K_G2, j, d, xid(d))

    def cp_g2v(j, d, w=False):
        return rc(TGX.at[j], tg_out.at[1, :, hcol(j, ry(-d) if w else y)], K_G2, j, 4 + d, yid(d))

    def cp_r(d, w=False):
        return rc1(RT, RTX.at[span(24 + 24 * (ry(-d) if w else y), 24, 8), :], O_R, d, yid(d))

    def cp_rh(d, w=False):
        if d == 1:
            return rc1(RTX.at[pl.ds(96, 24), :], RTX.at[pl.ds(0, 24), :], O_RH, 1, xid(1))
        return rc1(RTX.at[pl.ds(24, 24), :], RTX.at[pl.ds(120, 24), :], O_RH, 3, xid(3))

    def cp_mh(d, w=False):
        k = 1 if d == 1 else 0
        return rc1(MHS.at[k], MHR.at[1 - k], O_MH, d, xid(d))

    def cp_m(d, w=False):
        return rc1(MT.at[span(24 * ry(d), 24, 8), :], MR.at[ry(-d) if w else y], O_M, d, yid(d))

    def lo_h(j):
        return pltpu.make_async_copy(hid.at[:, hcol(j, y)], HX.at[j, slab(y), :], loc.at[0, j])

    def lo_do(j):
        return pltpu.make_async_copy(do_in.at[:, hcol(j, y)], DO.at[j, oslab(y), :], loc.at[1, j])

    def lo_tx(j):
        return pltpu.make_async_copy(txt.at[:, block(x), wide(j)], T1.at[j, x], loc.at[2, j])

    def lo_att(j):
        return pltpu.make_async_copy(ATT.at[j, oslab(y), :], att_out.at[:, hcol(j, y)], loc.at[3, j])

    def lo_g2k(j):
        return pltpu.make_async_copy(TGY.at[j], tg_out.at[0, block(x), wide(j)], loc.at[4, j])

    def lo_g2v(j):
        return pltpu.make_async_copy(TGX.at[j], tg_out.at[1, :, hcol(j, y)], loc.at[5, j])

    ALL = (1, 3, 2)
    SIDES = (1, 3)

    def stage_a(j):
        lo_tx(j).wait()
        for d in ALL:
            cp_tx(j, d, True).wait_recv()
        for kv in range(2):
            part = jnp.zeros((BLK, NY * BLK), f32)
            for k in range(NX):
                part = part + T1[j, k, kv].astype(f32) * sel_ref[k : k + 1, :]
            TS[j, kv] = part.astype(bf16)
        T2[j, y] = TS[j, :, :, block(y)]
        for d in ALL:
            cp_ty(j, d).start()
        lo_h(j).wait()
        for d in ALL:
            cp_h(j, d, True).wait_recv()
        for d in SIDES:
            cp_halo(j, d).start()

    def stage_b(j):
        for d in ALL:
            cp_ty(j, d, True).wait_recv()
        for kv in range(2):
            part = jnp.zeros((BLK, BLK), f32)
            for k in range(NY):
                part = part + T2[j, k, kv].astype(f32) * sel_ref[NX + k : NX + k + 1, :BLK]
            T3[j, kv, block(x), :] = part.astype(bf16)
        for d in ALL:
            cp_tg(j, d).start()

    def stage_c(j):
        for d in SIDES:
            cp_halo(j, d, True).wait_recv()
        lo_do(j).wait()
        for d in ALL:
            cp_do(j, d, True).wait_recv()
            cp_tg(j, d, True).wait_recv()
        head = NY * j + y
        gq = gq_ref[pl.ds(head, 1), :]
        gk = gk_ref[pl.ds(head, 1), :]
        par = lax.rem(j, 2)

        def prep(b, _):
            rows = block(b)
            h = HX[j, rows, :].astype(f32)
            kn = (h * RB[rows, :]) * gk
            KA[rows, :BLK] = kn.astype(bf16)
            KT[:, rows] = kn.T.astype(bf16)
            VT[:BLK, rows] = h.T.astype(bf16)
            return 0

        lax.fori_loop(0, EXT // BLK, prep, 0)
        for b in range(TXT // BLK):
            rows = slice(EXT + b * BLK, EXT + (b + 1) * BLK)
            kn = T3[j, 0, b * BLK : (b + 1) * BLK, :]
            KA[rows, :BLK] = kn
            KT[:, rows] = kn.astype(f32).T.astype(bf16)
            VT[:BLK, rows] = T3[j, 1, b * BLK : (b + 1) * BLK, :].astype(f32).T.astype(bf16)

        def clear(b, _):
            rows = span(b * KC, KC, KC)
            DK[rows, :] = jnp.zeros((KC, BLK), f32)
            DV[rows, :] = jnp.zeros((KC, BLK), f32)
            return 0

        lax.fori_loop(0, KEYS // KC, clear, 0)

        def tile(u, _):
            q0 = u * QT
            qrows = span(q0, QT, QT)
            erows = span(SLAB + q0, QT, BLK)
            h = HX[j, erows, :].astype(f32)
            qn = ((h * RB[erows, :]) * gq).astype(bf16)
            QA[:, :BLK] = qn
            QA[:, BLK:] = qb_ref[qrows, :]
            qa = QA[...]
            chunks = [span(q0 + KC * c, KC, KC) for c in range(4)]
            chunks += [pl.ds(EXT + KC * c, KC) for c in range(TXT // KC)]
            top = None
            for c in range(NCHUNK):
                s = dot_nt(KA[chunks[c], :], qa)
                S[c] = s
                high = jnp.max(s, axis=0, keepdims=True)
                top = high if top is None else jnp.maximum(top, high)
            top = top * (SCALE * LOG2E)
            ot = None
            for c in range(NCHUNK):
                p = jnp.exp2(S[c] * (SCALE * LOG2E) - top).astype(bf16)
                PB[c] = p
                term = dot_nn(VT[:, chunks[c]], p)
                ot = term if ot is None else ot + term
            inv = 1.0 / ot[BLK : BLK + 1, :]
            o = ot[:BLK, :] * inv
            dt = DO[j, qrows, :].astype(f32).T
            delta = jnp.sum(dt * o, axis=0, keepdims=True) * inv
            dts = (dt * inv).astype(bf16)
            ATT[j, qrows, :] = o.T.astype(bf16)
            dq = None
            for c in range(NCHUNK):
                if c < 4:
                    v = HX[j, chunks[c], :]
                else:
                    v = T3[j, 1, (c - 4) * KC : (c - 3) * KC, :]
                p = PB[c]
                dp = dot_nn(v, dts)
                ds = (p.astype(f32) * (dp - delta)).astype(bf16)
                DV[chunks[c], :] += dot_nt(p, dts)
                DK[chunks[c], :] += dot_nn(ds, qn)
                term = dot_nn(KT[:, chunks[c]], ds)
                dq = term if dq is None else dq + term
            DQ[qrows, :] = dq.T
            return 0

        lax.fori_loop(0, OWN // QT, tile, 0)

        for d in ALL:
            cp_att(j, d).start()
        lo_att(j).start()

        for k in range(2):
            rows = slice(k * (OWN + SLAB), k * (OWN + SLAB) + SLAB)
            r = RB[rows, :]
            t = (gk * DK[rows, :]) * SCALE
            AH[j, k] = (DV[rows, :] + r * t).astype(bf16)
            MH[k] += (HX[j, rows, :].astype(f32) * r) * t
        for d in SIDES:
            cp_ah(j, d).start()
        TGP[j, 0] = (DK[EXT:, :] * SCALE).astype(bf16)
        TGP[j, 1] = DV[EXT:, :].astype(bf16)
        TG1[j, x] = TGP[j, :, block(x), :]
        for d in ALL:
            cp_rs(j, d).start()

        def own(i, _):
            rows = slab(i)
            qrows = oslab(i)
            r = RB[rows, :]
            t = (gq * DQ[qrows, :] + gk * DK[rows, :]) * SCALE
            AFS[par, qrows, :] = DV[rows, :] + r * t
            M[qrows, :] += (HX[j, rows, :].astype(f32) * r) * t
            return 0

        lax.fori_loop(0, NY, own, 0)

    def stage_d(j):
        par = lax.rem(j, 2)
        for d in SIDES:
            cp_ah(j, d, True).wait_recv()
        for i in range(NY):
            rows = slice(i * SLAB, (i + 1) * SLAB)
            a = AFS[par, rows, :]
            if i == 0:
                a = a + AHR[j, 0].astype(f32)
            if i == NY - 1:
                a = a + AHR[j, 1].astype(f32)
            AO[j, rows, :] = a.astype(bf16)
        for d in ALL:
            cp_a(j, d).start()
        AF[:, hcol(j, y)] = AO[j, oslab(y), :]
        for d in ALL:
            cp_rs(j, d, True).wait_recv()
        for kv in range(2):
            total = TG1[j, 0, kv].astype(f32)
            for k in range(1, NX):
                total = total + TG1[j, k, kv].astype(f32)
            TG2[j, kv] = total.astype(bf16)
        TGY[j, :, block(y)] = TG2[j, 0]
        TGX[j, block(x), :] = TG2[j, 1]
        for d in ALL:
            cp_g1k(j, d).start()
            cp_g1v(j, d).start()

    def stage_e(j):
        for d in ALL:
            cp_g1k(j, d, True).wait_recv()
            cp_g1v(j, d, True).wait_recv()
        for d in ALL:
            cp_g2k(j, d).start()
            cp_g2v(j, d).start()
        lo_g2k(j).start()
        lo_g2v(j).start()

    barrier = pltpu.get_barrier_semaphore()
    for d in ALL:
        pl.semaphore_signal(barrier, inc=1, device_id=yid(d), device_id_type=MESH)
        pl.semaphore_signal(barrier, inc=1, device_id=xid(d), device_id_type=MESH)
    load = pltpu.make_async_copy(hid, HS, loc1.at[0])
    load.start()

    def first_local(j, _):
        lo_h(j).start()
        lo_tx(j).start()
        lo_do(j).start()
        return 0

    lax.fori_loop(0, STEPS, first_local, 0)
    pl.semaphore_wait(barrier, 6)

    def first(j, _):
        for d in ALL:
            cp_tx(j, d).start()
            cp_h(j, d).start()
        for d in ALL:
            cp_do(j, d).start()
        return 0

    lax.fori_loop(0, STEPS, first, 0)

    lane = lax.broadcasted_iota(jnp.int32, (BLK, BLK), 1)

    def marks(b, _):
        KA[block(b), BLK:] = jnp.where(lane == b, 1.0, 0.0).astype(bf16)
        return 0

    lax.fori_loop(0, EXT // BLK, marks, 0)
    KA[EXT:, BLK:] = jnp.zeros((TXT, BLK), bf16)
    VT[BLK:, :] = jnp.ones((16, KEYS), bf16)

    def clear_m(i, _):
        M[oslab(i), :] = jnp.zeros((SLAB, BLK), f32)
        return 0

    lax.fori_loop(0, NY, clear_m, 0)
    for k in range(2):
        MH[k] = jnp.zeros((SLAB, BLK), f32)

    load.wait()

    for b in range(SLAB // BLK):
        h = HS[b * BLK : (b + 1) * BLK, :].astype(f32)
        mean = jnp.sum(h * h, axis=1, keepdims=True) * (1.0 / WIDTH)
        RT[8 * b : 8 * b + 8, :] = packed(lax.rsqrt(mean + EPS))[0]
    for d in ALL:
        cp_r(d).start()
    RTX[span(24 + 24 * y, 24, 8), :] = RT[...]
    for d in ALL:
        cp_r(d, True).wait_recv()
    for d in SIDES:
        cp_rh(d).start()
    for d in SIDES:
        cp_rh(d, True).wait_recv()
    for b in range(EXT // BLK):
        RB[b * BLK : (b + 1) * BLK, :] = unpacked(RTX[8 * b : 8 * b + 8, :])

    stage_a(0)
    stage_b(0)
    stage_a(1)

    def step(j, _):
        stage_c(j)

        @pl.when(j + 1 < STEPS)
        def _():
            stage_b(j + 1)

        @pl.when(j + 2 < STEPS)
        def _():
            stage_a(j + 2)

        @pl.when(j >= 1)
        def _():
            stage_d(j - 1)

        @pl.when(j >= 2)
        def _():
            stage_e(j - 2)

        return 0

    lax.fori_loop(0, STEPS, step, 0)

    for k in range(2):
        tiles = packed(jnp.sum(MH[k], axis=1, keepdims=True))
        for b in range(SLAB // BLK):
            MHS[k, 8 * b : 8 * b + 8, :] = tiles[b]
    for d in SIDES:
        cp_mh(d).start()
    for b in range(OWN // BLK):
        column = jnp.sum(M[b * BLK : (b + 1) * BLK, :], axis=1, keepdims=True)
        MT[8 * b : 8 * b + 8, :] = packed(column)[0]
    stage_d(STEPS - 1)
    for d in SIDES:
        cp_mh(d, True).wait_recv()
    MT[:24, :] += MHR[0]
    MT[72:96, :] += MHR[1]
    for d in ALL:
        cp_m(d).start()
    MR[y] = MT[span(24 * y, 24, 8), :]
    stage_e(STEPS - 2)
    for d in ALL:
        cp_m(d, True).wait_recv()

    def arrived(j, _):
        for d in ALL:
            cp_a(j, d, True).wait_recv()
        return 0

    lax.fori_loop(0, STEPS, arrived, 0)
    for b in range(SLAB // BLK):
        rows = slice(b * BLK, (b + 1) * BLK)
        tiles = slice(8 * b, 8 * b + 8)
        mean = (MR[0, tiles] + MR[1, tiles] + MR[2, tiles] + MR[3, tiles]) * (1.0 / WIDTH)
        r = RT[tiles, :]
        factor = unpacked(mean * (r * r))[:, :1]
        DH[rows, :] = (AF[rows, :].astype(f32) - HS[rows, :].astype(f32) * factor).astype(bf16)
    store = pltpu.make_async_copy(DH, dh_out, loc1.at[1])
    store.start()
    stage_e(STEPS - 1)
    store.wait()

    def last(j, _):
        for d in ALL:
            cp_att(j, d, True).wait_recv()
            cp_g2k(j, d, True).wait_recv()
            cp_g2v(j, d, True).wait_recv()
            for copy in (cp_h, cp_do, cp_tx, cp_ty, cp_tg, cp_att, cp_a, cp_rs, cp_g1k, cp_g1v, cp_g2k, cp_g2v):
                copy(j, d).wait_send()
        for d in SIDES:
            cp_halo(j, d).wait_send()
            cp_ah(j, d).wait_send()
        lo_att(j).wait()
        lo_g2k(j).wait()
        lo_g2v(j).wait()
        return 0

    lax.fori_loop(0, STEPS, last, 0)
    for d in ALL:
        cp_r(d).wait_send()
        cp_m(d).wait_send()
    for d in SIDES:
        cp_rh(d).wait_send()
        cp_mh(d).wait_send()


def query_bias(pattern, x):
    blocks = OWN // BLK
    reach = SLAB // BLK
    span_ = pattern.shape[1]
    rows = lax.dynamic_slice_in_dim(pattern, x * blocks, blocks, 0)
    first = jnp.arange(blocks, dtype=jnp.int32)[:, None]
    col = jnp.arange(BLK, dtype=jnp.int32)[None, :]
    offset = col - first
    onehot = offset[:, :, None] == jnp.arange(span_, dtype=jnp.int32)[None, None, :]
    picked = jnp.sum(jnp.where(onehot, rows[:, None, :], 0), axis=-1)
    globe = x * blocks - reach + col
    inside = (globe >= 0) & (globe < pattern.shape[0])
    allowed = ((picked > 0) & inside) | (col >= EXT // BLK)
    return jnp.repeat(jnp.where(allowed, 0.0, NEG).astype(bf16), BLK, axis=0)


def shifted(x, axis, by):
    peers = lax.axis_size(axis)
    pairs = [(i, i + by) for i in range(peers) if 0 <= i + by < peers]
    return lax.ppermute(x, axis, pairs)


def local(hidden, query_norm_gain, key_norm_gain, text_kv, holder, pattern, grad_out):
    x = lax.axis_index("seq") // NY
    qbias = query_bias(pattern, x)
    who = holder[0]
    select = jnp.concatenate([jnp.arange(NX) == who // NY, jnp.arange(NY) == who % NY])
    select = jnp.broadcast_to(select.astype(f32)[:, None], (NX + NY, NY * BLK))
    heads = WIDTH // HDIM
    any_spec = pl.BlockSpec(memory_space=pl.ANY)
    vmem = pl.BlockSpec(memory_space=pltpu.VMEM)

    def V(*shape, dtype=bf16):
        return pltpu.VMEM(shape, dtype)

    attended, grad_hidden, text_total = pl.pallas_call(
        kernel,
        out_shape=(
            jax.ShapeDtypeStruct((SLAB, WIDTH), bf16),
            jax.ShapeDtypeStruct((SLAB, WIDTH), bf16),
            jax.ShapeDtypeStruct((2, TXT, WIDTH), bf16),
        ),
        in_specs=[any_spec] * 3 + [vmem] * 4,
        out_specs=[any_spec] * 3,
        scratch_shapes=[
            V(SLAB, WIDTH),
            V(STEPS, EXT, BLK),
            V(STEPS, OWN, BLK),
            V(EXT // BLK * 8, BLK, dtype=f32),
            V(24, BLK, dtype=f32),
            V(EXT, BLK, dtype=f32),
            V(STEPS, NX, 2, BLK, NY * BLK),
            V(STEPS, 2, BLK, NY * BLK),
            V(STEPS, NY, 2, BLK, BLK),
            V(STEPS, 2, TXT, BLK),
            V(KEYS, 2 * BLK),
            V(BLK, KEYS),
            V(BLK + 16, KEYS),
            V(QT, 2 * BLK),
            V(NCHUNK, KC, QT, dtype=f32),
            V(NCHUNK, KC, QT),
            V(KEYS, BLK, dtype=f32),
            V(KEYS, BLK, dtype=f32),
            V(OWN, BLK, dtype=f32),
            V(STEPS, OWN, BLK),
            V(2, OWN, BLK, dtype=f32),
            V(STEPS, 2, SLAB, BLK),
            V(STEPS, 2, SLAB, BLK),
            V(STEPS, OWN, BLK),
            V(SLAB, WIDTH),
            V(OWN, BLK, dtype=f32),
            V(2, SLAB, BLK, dtype=f32),
            V(96, BLK, dtype=f32),
            V(2, 24, BLK, dtype=f32),
            V(2, 24, BLK, dtype=f32),
            V(NY, 24, BLK, dtype=f32),
            V(STEPS, 2, TXT, BLK),
            V(STEPS, NX, 2, BLK, BLK),
            V(STEPS, 2, BLK, BLK),
            V(STEPS, BLK, NY * BLK),
            V(STEPS, TXT, BLK),
            V(SLAB, WIDTH),
            pltpu.SemaphoreType.DMA((KINDS, STEPS, 8)),
            pltpu.SemaphoreType.DMA((KINDS, STEPS, 8)),
            pltpu.SemaphoreType.DMA((4, 4)),
            pltpu.SemaphoreType.DMA((4, 4)),
            pltpu.SemaphoreType.DMA((6, STEPS)),
            pltpu.SemaphoreType.DMA((2,)),
        ],
        compiler_params=pltpu.CompilerParams(
            collective_id=0, has_side_effects=True, vmem_limit_bytes=60 * 1024 * 1024
        ),
        cost_estimate=pl.CostEstimate(
            flops=24 * 10**9, bytes_accessed=40 * 10**6, transcendentals=12 * 10**6
        ),
        name="attention",
    )(
        hidden[0],
        grad_out[0],
        text_kv[0, 0],
        query_norm_gain.reshape(heads, HDIM),
        key_norm_gain.reshape(heads, HDIM),
        select,
        qbias,
    )
    upstream = shifted(grad_hidden, "section", -1)
    return (attended[None], upstream[None], text_total[None])


def solution(mesh):
    in_specs = (
        P("section", "seq", None),
        P("section", None),
        P("section", None),
        P("section", "seq", None, None, None),
        P("section"),
        P(),
        P("section", "seq", None),
    )
    out_specs = (
        P("section", "seq", None),
        P("section", "seq", None),
        P("section", None, None, None),
    )
    return jax.shard_map(local, mesh=mesh, in_specs=in_specs, out_specs=out_specs, check_vma=False)
```

time: 929 us -> 260 us (0.28)
  matrix products: 237 us -> 0 us
  blocking collectives: 234 us -> 0 us
  Pallas kernels: 0 us -> 209 us
  waiting for transfers between devices: 180 us -> 24 us
  local copies, waits for them, and re-layouts: 158 us -> 8.38 us
  other arithmetic: 79 us -> 2.85 us
  between operations: 14.9 us -> 1.42 us
    dot_general x120 -> x0, matrix products: 237 us -> none  [the longest x20 51.2 us: query_side(): dvals = jnp.dot(probs_b.T, doh, preferred_element_type=jnp.float32)]
    psum x1 -> x0, blocking collectives: 234 us -> none  [local(): text_total = lax.psum(dtext_part, 'seq')]
    pallas_call x0 -> x1, Pallas kernels: none -> 209 us  [local(): pl.pallas_call(kernel, out_shape=(jax.ShapeDtypeStruct((SLAB, WIDTH), bf1...]
    ppermute x2 -> x0, waiting for transfers between devices: 92 us -> none  [the longest x1 89.1 us: extended(): lax.ppermute(head, axis, [((i + 1) % count, i) for i in range(ends)])]
    dynamic_slice x122 -> x2, local copies, waits for them, and re-layouts: 68.3 us -> 0.17 us  [query_bias(): rows = lax.dynamic_slice_in_dim(pattern, x * blocks, blocks, 0)]
    slice x7 -> x0, local copies, waits for them, and re-layouts: 44.4 us -> none  [the longest x1 9.75 us: local(): dkeys[:, :ext_rows]]
    reduce_sum x44 -> x1, other arithmetic: 37.7 us -> 0.09 us  [query_bias(): picked = jnp.sum(jnp.where(onehot, rows[:, None, :], 0), axis=-1)]
    ppermute x3 -> x1, waiting for transfers between devices: 56.4 us -> 24 us  [shifted(): return lax.ppermute(x, axis, pairs)]
  transfers between devices with their start and end apart: 6 -> 1, of which waited for: 5 -> 1; matrix products, arithmetic and copies ran while one was open for 7% -> 0% of each run, Pallas kernels for 0% -> 0%
where the time goes in v1:
time: 260 us; the launch traced here: 259 us
  Pallas kernels  209 us (80%)
  waiting for transfers between devices  24 us (9%)
  starting transfers between devices  13.8 us (5%)
  local copies, waits for them, and re-layouts  8.38 us (3%)
  other arithmetic  2.85 us (1%)
    pallas_call x1, Pallas kernels, local(): pl.pallas_call(kernel, out_shape=(jax.ShapeDtypeStruct((SLAB, WIDTH), bf1...  209 us
    ppermute x1, waiting for transfers between devices, shifted(): return lax.ppermute(x, axis, pairs)  24 us
    ppermute x1, starting transfers between devices, shifted(): return lax.ppermute(x, axis, pairs)  13.8 us
    unnamed x7, local copies, waits for them, and re-layouts  6.73 us
  transfers between devices with their start and end apart: 1, of which 1 were waited for; matrix products, arithmetic and copies ran while one was open for 0% of the time, Pallas kernels for 0%

profile of v1, /device:TPU:1, one launch (start us, length us, event | category | flops | bytes accessed | tf_op | source)
XLA Modules:
  0.0 259.5 jit_solution(5537713243645165408)
XLA Ops:
  0.6 0.0 copy-start
  1.4 0.0 copy-done
  1.4 0.1 constant_dynamic-slice_fusion
  1.5 0.1 copy.11
  1.6 1.3 reduce
  2.9 1.3 reduce.1
  4.2 0.1 add_convert_fusion
  4.3 0.1 select_reduce_fusion
  4.4 0.7 broadcast_in_dim.43.sel_ref
  5.1 0.8 broadcast_in_dim.48
  5.9 209.1 %attention.1 = (bf16[384,2560]{1,0:T(8,128)(2,1)}, bf16[384,2560]{1,0:T(8,128)(2,1)}, bf16[2,512,2560]{2,1,0:T(8,128)(2,1)}) custom-call(bf16[384,2560]{1,0:T(8,128)(2,1)} %bitcast.21, bf16[384,2560]{1,0:T(8,128)(2,1)} %bitcast.22, bf16[2,512,2560]{2,1,0:T(8,128)(2,1)} %bitcast.20, f32[20,128]{1,0:T(8,128)} %bitcast.18, f32[20,128]{1,0:T(8,128)} %bitcast.19, ...), custom_call_target="tpu_custom_call" | custom-call | flops 24000000000 | bytes 40000000 | tf_op jit(solution)/shard_map/attention/pallas_call | solution.py:572
  215.0 13.8 %collective-permute-start = (bf16[384,2560]{1,0:T(8,128)(2,1)}, bf16[384,2560]{1,0:T(8,128)(2,1)S(1)}, u32[]{:S(2)}, u32[]{:S(2)}) collective-permute-start(bf16[384,2560]{1,0:T(8,128)(2,1)} %get-tuple-element.7), channel_id=1, source_target_pairs={{1,0},{2,1},{3,2},{4,3},{5,4},{6,5},{7,6},{9,8},{10,9},{11,10},{12... | collective-permute-start | bytes 5898248 | tf_op jit(solution)/shard_map/ppermute | solution.py:556
  228.8 24.0 %collective-permute-done = bf16[384,2560]{1,0:T(8,128)(2,1)S(1)} collective-permute-done((bf16[384,2560]{1,0:T(8,128)(2,1)}, bf16[384,2560]{1,0:T(8,128)(2,1)S(1)}, u32[]{:S(2)}, u32[]{:S(2)}) %collective-permute-start) | collective-permute-done | bytes 1966112 | tf_op jit(solution)/shard_map/ppermute | solution.py:556
  252.8 0.0 copy-start.1
  252.8 3.1 %copy.16 = bf16[1,384,2560]{2,1,0:T(8,128)(2,1)} copy(bf16[1,384,2560]{2,1,0:T(8,128)(2,1)} %bitcast.15) | data formatting | bytes 3932160
  255.9 1.3 copy.17
  257.1 0.0 copy-done.1
  257.1 2.4 copy.18
  (4 shorter events, 0.0 us)
Async XLA Ops:
  0.6 0.8 copy-start
  215.0 37.8 %collective-permute-start = (bf16[384,2560]{1,0:T(8,128)(2,1)}, bf16[384,2560]{1,0:T(8,128)(2,1)S(1)}, u32[]{:S(2)}, u32[]{:S(2)}) collective-permute-start(bf16[384,2560]{1,0:T(8,128)(2,1)} %get-tuple-element.7), channel_id=1, source_target_pairs={{1,0},{2,1},{3,2},{4,3},{5,4},{6,5},{7,6},{9,8},{10,9},{11,10},{12... | collective-permute-start | bytes 5898248 | tf_op jit(solution)/shard_map/ppermute | solution.py:556
  252.8 4.4 %copy-start.1 = (bf16[2,512,2560]{2,1,0:T(8,128)(2,1)S(1)}, bf16[2,512,2560]{2,1,0:T(8,128)(2,1)}, u32[]{:S(2)}) copy-start(bf16[2,512,2560]{2,1,0:T(8,128)(2,1)} %get-tuple-element.8) | copy-start | bytes 15728644

commit v2 on v1

--- a/solution.py
+++ b/solution.py
@@ -41,7 +41,7 @@
     K_G2,
 ) = range(12)
 KINDS = 12
-O_R, O_RH, O_MH, O_M = range(4)
+O_R, O_RH, O_MH, O_M, O_HU = range(5)
 
 f32 = jnp.float32
 bf16 = jnp.bfloat16
@@ -76,11 +76,13 @@
 def kernel(
     hid, do_in, txt, gq_ref, gk_ref, sel_ref, qb_ref,
     att_out, dh_out, tg_out,
-    HS, HX, DO, RTX, RT, RB, T1, TS, T2, T3, KA, KT, VT, QA, S, PB, DK, DV, DQ,
+    HS, HU, RU, HX, DO, RTX, RT, RB, T1, TS, T2, T3, KA, KT, VT, QA, S, PB, DK, DV, DQ,
     ATT, AFS, AH, AHR, AO, AF, M, MH, MT, MHS, MHR, MR, TGP, TG1, TG2, TGY, TGX, DH,
     send, recv, once_send, once_recv, loc, loc1,
 ):
     seq = lax.axis_index("seq")
+    section = lax.axis_index("section")
+    sections = lax.axis_size("section")
     x = lax.div(seq, NY)
     y = lax.rem(seq, NY)
 
@@ -95,6 +97,12 @@
 
     def xid(d):
         return {"seq": rx(d) * NY + y}
+
+    def below(d):
+        return {"seq": x * NY + ry(d), "section": lax.rem(section + (sections - 1), sections)}
+
+    def above(d):
+        return {"seq": x * NY + ry(d), "section": lax.rem(section + 1, sections)}
 
     def rc(src, dst, kind, j, d, dev):
         return pltpu.make_async_remote_copy(
@@ -148,7 +156,7 @@
         return rc(AH.at[j, k], AHR.at[j, 1 - k], K_AH, j, d, xid(d))
 
     def cp_a(j, d, w=False):
-        return rc(AO.at[j, oslab(ry(d)), :], AF.at[:, hcol(j, ry(-d) if w else y)], K_A, j, d, yid(d))
+        return rc(AO.at[j, oslab(ry(d)), :], AF.at[:, hcol(j, ry(-d) if w else y)], K_A, j, d, below(d))
 
     def cp_rs(j, d, w=False):
         return rc(TGP.at[j, :, block(rx(d)), :], TG1.at[j, rx(-d) if w else x], K_RS, j, d, xid(d))
@@ -178,7 +186,13 @@
         return rc1(MHS.at[k], MHR.at[1 - k], O_MH, d, xid(d))
 
     def cp_m(d, w=False):
-        return rc1(MT.at[span(24 * ry(d), 24, 8), :], MR.at[ry(-d) if w else y], O_M, d, yid(d))
+        return rc1(MT.at[span(24 * ry(d), 24, 8), :], MR.at[ry(-d) if w else y], O_M, d, below(d))
+
+    def cp_hu():
+        return rc1(hid, HU, O_HU, 0, below(0))
+
+    def cp_ru():
+        return rc1(RT, RU, O_HU, 1, below(0))
 
     def lo_h(j):
         return pltpu.make_async_copy(hid.at[:, hcol(j, y)], HX.at[j, slab(y), :], loc.at[0, j])
@@ -199,7 +213,15 @@
         return pltpu.make_async_copy(TGX.at[j], tg_out.at[1, :, hcol(j, y)], loc.at[5, j])
 
     ALL = (1, 3, 2)
+    FOUR = (0, 1, 3, 2)
     SIDES = (1, 3)
+
+    def front(j):
+        for d in ALL:
+            cp_tx(j, d).start()
+            cp_h(j, d).start()
+        for d in ALL:
+            cp_do(j, d).start()
 
     def stage_a(j):
         lo_tx(j).wait()
@@ -356,9 +378,8 @@
             if i == NY - 1:
                 a = a + AHR[j, 1].astype(f32)
             AO[j, rows, :] = a.astype(bf16)
-        for d in ALL:
+        for d in FOUR:
             cp_a(j, d).start()
-        AF[:, hcol(j, y)] = AO[j, oslab(y), :]
         for d in ALL:
             cp_rs(j, d, True).wait_recv()
         for kv in range(2):
@@ -386,6 +407,8 @@
     for d in ALL:
         pl.semaphore_signal(barrier, inc=1, device_id=yid(d), device_id_type=MESH)
         pl.semaphore_signal(barrier, inc=1, device_id=xid(d), device_id_type=MESH)
+    for d in FOUR:
+        pl.semaphore_signal(barrier, inc=1, device_id=above(d), device_id_type=MESH)
     load = pltpu.make_async_copy(hid, HS, loc1.at[0])
     load.start()
 
@@ -396,17 +419,10 @@
         return 0
 
     lax.fori_loop(0, STEPS, first_local, 0)
-    pl.semaphore_wait(barrier, 6)
-
-    def first(j, _):
-        for d in ALL:
-            cp_tx(j, d).start()
-            cp_h(j, d).start()
-        for d in ALL:
-            cp_do(j, d).start()
-        return 0
-
-    lax.fori_loop(0, STEPS, first, 0)
+    pl.semaphore_wait(barrier, 10)
+
+    front(0)
+    cp_hu().start()
 
     lane = lax.broadcasted_iota(jnp.int32, (BLK, BLK), 1)
 
@@ -434,6 +450,7 @@
         RT[8 * b : 8 * b + 8, :] = packed(lax.rsqrt(mean + EPS))[0]
     for d in ALL:
         cp_r(d).start()
+    cp_ru().start()
     RTX[span(24 + 24 * y, 24, 8), :] = RT[...]
     for d in ALL:
         cp_r(d, True).wait_recv()
@@ -441,15 +458,20 @@
         cp_rh(d).start()
     for d in SIDES:
         cp_rh(d, True).wait_recv()
+    stage_a(0)
+    front(1)
     for b in range(EXT // BLK):
         RB[b * BLK : (b + 1) * BLK, :] = unpacked(RTX[8 * b : 8 * b + 8, :])
-
-    stage_a(0)
     stage_b(0)
+    front(2)
     stage_a(1)
 
     def step(j, _):
         stage_c(j)
+
+        @pl.when(j + 3 < STEPS)
+        def _():
+            front(j + 3)
 
         @pl.when(j + 1 < STEPS)
         def _():
@@ -485,15 +507,16 @@
         cp_mh(d, True).wait_recv()
     MT[:24, :] += MHR[0]
     MT[72:96, :] += MHR[1]
-    for d in ALL:
+    for d in FOUR:
         cp_m(d).start()
-    MR[y] = MT[span(24 * y, 24, 8), :]
     stage_e(STEPS - 2)
-    for d in ALL:
+    cp_hu().wait_recv()
+    cp_ru().wait_recv()
+    for d in FOUR:
         cp_m(d, True).wait_recv()
 
     def arrived(j, _):
-        for d in ALL:
+        for d in FOUR:
             cp_a(j, d, True).wait_recv()
         return 0
 
@@ -502,9 +525,10 @@
         rows = slice(b * BLK, (b + 1) * BLK)
         tiles = slice(8 * b, 8 * b + 8)
         mean = (MR[0, tiles] + MR[1, tiles] + MR[2, tiles] + MR[3, tiles]) * (1.0 / WIDTH)
-        r = RT[tiles, :]
+        r = RU[tiles, :]
         factor = unpacked(mean * (r * r))[:, :1]
-        DH[rows, :] = (AF[rows, :].astype(f32) - HS[rows, :].astype(f32) * factor).astype(bf16)
+        grad = AF[rows, :].astype(f32) - HU[rows, :].astype(f32) * factor
+        DH[rows, :] = jnp.where(section < sections - 1, grad, 0.0).astype(bf16)
     store = pltpu.make_async_copy(DH, dh_out, loc1.at[1])
     store.start()
     stage_e(STEPS - 1)
@@ -515,8 +539,10 @@
             cp_att(j, d, True).wait_recv()
             cp_g2k(j, d, True).wait_recv()
             cp_g2v(j, d, True).wait_recv()
-            for copy in (cp_h, cp_do, cp_tx, cp_ty, cp_tg, cp_att, cp_a, cp_rs, cp_g1k, cp_g1v, cp_g2k, cp_g2v):
+            for copy in (cp_h, cp_do, cp_tx, cp_ty, cp_tg, cp_att, cp_rs, cp_g1k, cp_g1v, cp_g2k, cp_g2v):
                 copy(j, d).wait_send()
+        for d in FOUR:
+            cp_a(j, d).wait_send()
         for d in SIDES:
             cp_halo(j, d).wait_send()
             cp_ah(j, d).wait_send()
@@ -528,7 +554,10 @@
     lax.fori_loop(0, STEPS, last, 0)
     for d in ALL:
         cp_r(d).wait_send()
+    for d in FOUR:
         cp_m(d).wait_send()
+    cp_hu().wait_send()
+    cp_ru().wait_send()
     for d in SIDES:
         cp_rh(d).wait_send()
         cp_mh(d).wait_send()
@@ -550,12 +579,6 @@
     return jnp.repeat(jnp.where(allowed, 0.0, NEG).astype(bf16), BLK, axis=0)
 
 
-def shifted(x, axis, by):
-    peers = lax.axis_size(axis)
-    pairs = [(i, i + by) for i in range(peers) if 0 <= i + by < peers]
-    return lax.ppermute(x, axis, pairs)
-
-
 def local(hidden, query_norm_gain, key_norm_gain, text_kv, holder, pattern, grad_out):
     x = lax.axis_index("seq") // NY
     qbias = query_bias(pattern, x)
@@ -569,7 +592,7 @@
     def V(*shape, dtype=bf16):
         return pltpu.VMEM(shape, dtype)
 
-    attended, grad_hidden, text_total = pl.pallas_call(
+    attended, upstream, text_total = pl.pallas_call(
         kernel,
         out_shape=(
             jax.ShapeDtypeStruct((SLAB, WIDTH), bf16),
@@ -580,6 +603,8 @@
         out_specs=[any_spec] * 3,
         scratch_shapes=[
             V(SLAB, WIDTH),
+            V(SLAB, WIDTH),
+            V(24, BLK, dtype=f32),
             V(STEPS, EXT, BLK),
             V(STEPS, OWN, BLK),
             V(EXT // BLK * 8, BLK, dtype=f32),
@@ -618,8 +643,8 @@
             V(SLAB, WIDTH),
             pltpu.SemaphoreType.DMA((KINDS, STEPS, 8)),
             pltpu.SemaphoreType.DMA((KINDS, STEPS, 8)),
-            pltpu.SemaphoreType.DMA((4, 4)),
-            pltpu.SemaphoreType.DMA((4, 4)),
+            pltpu.SemaphoreType.DMA((5, 4)),
+            pltpu.SemaphoreType.DMA((5, 4)),
             pltpu.SemaphoreType.DMA((6, STEPS)),
             pltpu.SemaphoreType.DMA((2,)),
         ],
@@ -639,7 +664,6 @@
         select,
         qbias,
     )
-    upstream = shifted(grad_hidden, "section", -1)
     return (attended[None], upstream[None], text_total[None])
 
 

time: 260 us -> 221 us (0.85)
  waiting for transfers between devices: 24 us -> 0 us
  starting transfers between devices: 13.8 us -> 0 us
  Pallas kernels: 209 us -> 206 us
    ppermute x1 -> x0, waiting for transfers between devices: 24 us -> none  [shifted(): return lax.ppermute(x, axis, pairs)]
    ppermute x1 -> x0, starting transfers between devices: 13.8 us -> none  [shifted(): return lax.ppermute(x, axis, pairs)]
    pallas_call x1, Pallas kernels: 209 us -> 206 us  [local(): pl.pallas_call(kernel, out_shape=(jax.ShapeDtypeStruct((SLAB, WIDTH), bf1...]
  transfers between devices with their start and end apart: 1 -> 0, of which waited for: 1 -> 0; matrix products, arithmetic and copies ran while one was open for 0% -> 0% of each run, Pallas kernels for 0% -> 0%
where the time goes in v2:
time: 221 us
  Pallas kernels  206 us (93%)
  local copies, waits for them, and re-layouts  10.1 us (5%)
  other arithmetic  2.85 us (1%)
    pallas_call x1, Pallas kernels, local(): pl.pallas_call(kernel, out_shape=(jax.ShapeDtypeStruct((SLAB, WIDTH), bf1...  206 us
    unnamed x7, local copies, waits for them, and re-layouts  8.41 us

profile of v2, /device:TPU:1, one launch (start us, length us, event | category | flops | bytes accessed | tf_op | source)
XLA Modules:
  0.0 220.6 jit_solution(14636321621958074537)
XLA Ops:
  0.6 0.0 copy-start
  1.4 0.1 add_convert_fusion
  1.4 0.0 copy-done
  1.4 0.1 constant_dynamic-slice_fusion
  1.5 0.1 copy.11
  1.6 0.1 select_reduce_fusion
  1.7 1.3 reduce
  3.1 1.3 reduce.1
  4.4 0.7 broadcast_in_dim.43.sel_ref
  5.1 0.8 broadcast_in_dim.48
  5.9 206.3 %attention.1 = (bf16[384,2560]{1,0:T(8,128)(2,1)}, bf16[384,2560]{1,0:T(8,128)(2,1)}, bf16[2,512,2560]{2,1,0:T(8,128)(2,1)}) custom-call(bf16[384,2560]{1,0:T(8,128)(2,1)} %bitcast.21, bf16[384,2560]{1,0:T(8,128)(2,1)} %bitcast.22, bf16[2,512,2560]{2,1,0:T(8,128)(2,1)} %bitcast.20, f32[20,128]{1,0:T(8,128)} %bitcast.18, f32[20,128]{1,0:T(8,128)} %bitcast.19, ...), custom_call_target="tpu_custom_call" | custom-call | flops 24000000000 | bytes 40000000 | tf_op jit(solution)/shard_map/attention/pallas_call | solution.py:595
  212.2 0.0 copy-start.1
  212.2 3.1 %copy.16 = bf16[1,384,2560]{2,1,0:T(8,128)(2,1)} copy(bf16[1,384,2560]{2,1,0:T(8,128)(2,1)} %bitcast.16) | data formatting | bytes 3932160
  215.3 2.9 %copy.17 = bf16[1,384,2560]{2,1,0:T(8,128)(2,1)} copy(bf16[1,384,2560]{2,1,0:T(8,128)(2,1)} %bitcast.15) | data formatting | bytes 3932160
  218.2 0.0 copy-done.1
  218.2 2.4 %copy.18 = bf16[1,2,512,2560]{3,2,1,0:T(8,128)(2,1)} copy(bf16[1,2,512,2560]{3,2,1,0:T(8,128)(2,1)S(1)} %bitcast.14) | data formatting | bytes 10485760
  (4 shorter events, 0.0 us)
Async XLA Ops:
  0.6 0.8 copy-start
  212.2 6.0 %copy-start.1 = (bf16[2,512,2560]{2,1,0:T(8,128)(2,1)S(1)}, bf16[2,512,2560]{2,1,0:T(8,128)(2,1)}, u32[]{:S(2)}) copy-start(bf16[2,512,2560]{2,1,0:T(8,128)(2,1)} %get-tuple-element.8) | copy-start | bytes 15728644

commit v3 on v2

--- a/solution.py
+++ b/solution.py
@@ -55,6 +55,14 @@
     return lax.dot_general(a, b, (((1,), (1,)), ((), ())), preferred_element_type=f32)
 
 
+def woven(*parts):
+    parts = list(parts)
+    while parts:
+        for part in list(parts):
+            if next(part, True):
+                parts.remove(part)
+
+
 def block(k):
     return pl.ds(pl.multiple_of(k * BLK, BLK), BLK)
 
@@ -76,10 +84,11 @@
 def kernel(
     hid, do_in, txt, gq_ref, gk_ref, sel_ref, qb_ref,
     att_out, dh_out, tg_out,
-    HS, HU, RU, HX, DO, RTX, RT, RB, T1, TS, T2, T3, KA, KT, VT, QA, S, PB, DK, DV, DQ,
+    HS, HU, RU, HX, DO, RTX, RT, RB, T1, TS, T2, T3, KA, KT, VT, QA0, QA1, S, PB0, PB1, DTS0, DTS1, DL0, DL1, DK, DV, DQ,
     ATT, AFS, AH, AHR, AO, AF, M, MH, MT, MHS, MHR, MR, TGP, TG1, TG2, TGY, TGX, DH,
     send, recv, once_send, once_recv, loc, loc1,
 ):
+    QA, PB, DTS, DL = (QA0, QA1), (PB0, PB1), (DTS0, DTS1), (DL0, DL1)
     seq = lax.axis_index("seq")
     section = lax.axis_index("section")
     sections = lax.axis_size("section")
@@ -252,7 +261,7 @@
         for d in ALL:
             cp_tg(j, d).start()
 
-    def stage_c(j):
+    def stage_c(j, between):
         for d in SIDES:
             cp_halo(j, d, True).wait_recv()
         lo_do(j).wait()
@@ -269,8 +278,8 @@
             h = HX[j, rows, :].astype(f32)
             kn = (h * RB[rows, :]) * gk
             KA[rows, :BLK] = kn.astype(bf16)
-            KT[:, rows] = kn.T.astype(bf16)
-            VT[:BLK, rows] = h.T.astype(bf16)
+            KT[:, rows] = kn.astype(bf16).T
+            VT[:BLK, rows] = HX[j, rows, :].T
             return 0
 
         lax.fori_loop(0, EXT // BLK, prep, 0)
@@ -278,8 +287,8 @@
             rows = slice(EXT + b * BLK, EXT + (b + 1) * BLK)
             kn = T3[j, 0, b * BLK : (b + 1) * BLK, :]
             KA[rows, :BLK] = kn
-            KT[:, rows] = kn.astype(f32).T.astype(bf16)
-            VT[:BLK, rows] = T3[j, 1, b * BLK : (b + 1) * BLK, :].astype(f32).T.astype(bf16)
+            KT[:, rows] = kn.T
+            VT[:BLK, rows] = T3[j, 1, b * BLK : (b + 1) * BLK, :].T
 
         def clear(b, _):
             rows = span(b * KC, KC, KC)
@@ -289,53 +298,79 @@
 
         lax.fori_loop(0, KEYS // KC, clear, 0)
 
-        def tile(u, _):
+        def chunks_of(q0):
+            chunks = [span(q0 + KC * c, KC, KC) for c in range(4)]
+            return chunks + [pl.ds(EXT + KC * c, KC) for c in range(TXT // KC)]
+
+        def forward(u, k):
             q0 = u * QT
             qrows = span(q0, QT, QT)
             erows = span(SLAB + q0, QT, BLK)
             h = HX[j, erows, :].astype(f32)
-            qn = ((h * RB[erows, :]) * gq).astype(bf16)
-            QA[:, :BLK] = qn
-            QA[:, BLK:] = qb_ref[qrows, :]
-            qa = QA[...]
-            chunks = [span(q0 + KC * c, KC, KC) for c in range(4)]
-            chunks += [pl.ds(EXT + KC * c, KC) for c in range(TXT // KC)]
+            QA[k][:, :BLK] = ((h * RB[erows, :]) * gq).astype(bf16)
+            for b in range(QT // BLK):
+                bias = qb_ref[pl.ds(u * (QT // BLK) + b, 1), :].astype(bf16)
+                QA[k][b * BLK : (b + 1) * BLK, BLK:] = jnp.broadcast_to(bias, (BLK, BLK))
+            qa = QA[k][...]
+            chunks = chunks_of(q0)
             top = None
             for c in range(NCHUNK):
                 s = dot_nt(KA[chunks[c], :], qa)
                 S[c] = s
                 high = jnp.max(s, axis=0, keepdims=True)
                 top = high if top is None else jnp.maximum(top, high)
+                yield
             top = top * (SCALE * LOG2E)
+            dt = DO[j, qrows, :].astype(f32).T
             ot = None
             for c in range(NCHUNK):
                 p = jnp.exp2(S[c] * (SCALE * LOG2E) - top).astype(bf16)
-                PB[c] = p
+                PB[k][c] = p
                 term = dot_nn(VT[:, chunks[c]], p)
                 ot = term if ot is None else ot + term
+                yield
             inv = 1.0 / ot[BLK : BLK + 1, :]
             o = ot[:BLK, :] * inv
-            dt = DO[j, qrows, :].astype(f32).T
             delta = jnp.sum(dt * o, axis=0, keepdims=True) * inv
-            dts = (dt * inv).astype(bf16)
+            DTS[k][...] = (dt * inv).astype(bf16)
+            DL[k][...] = jnp.broadcast_to(delta, (8, QT))
             ATT[j, qrows, :] = o.T.astype(bf16)
+
+        def backward(u, k):
+            q0 = u * QT
+            chunks = chunks_of(q0)
+            dts = DTS[k][...]
+            delta = DL[k][:1, :]
+            qn = QA[k][:, :BLK]
             dq = None
             for c in range(NCHUNK):
                 if c < 4:
                     v = HX[j, chunks[c], :]
                 else:
                     v = T3[j, 1, (c - 4) * KC : (c - 3) * KC, :]
-                p = PB[c]
+                p = PB[k][c]
                 dp = dot_nn(v, dts)
                 ds = (p.astype(f32) * (dp - delta)).astype(bf16)
                 DV[chunks[c], :] += dot_nt(p, dts)
+                yield
                 DK[chunks[c], :] += dot_nn(ds, qn)
                 term = dot_nn(KT[:, chunks[c]], ds)
                 dq = term if dq is None else dq + term
-            DQ[qrows, :] = dq.T
+                yield
+            DQ[span(q0, QT, QT), :] = dq.T
+
+        tiles = OWN // QT
+        woven(forward(0, 0))
+
+        def pair(v, _):
+            woven(forward(2 * v + 1, 1), backward(2 * v, 0))
+            woven(forward(2 * v + 2, 0), backward(2 * v + 1, 1))
+            between(v)
             return 0
 
-        lax.fori_loop(0, OWN // QT, tile, 0)
+        lax.fori_loop(0, tiles // 2 - 1, pair, 0)
+        woven(forward(tiles - 1, 1), backward(tiles - 2, 0))
+        woven(backward(tiles - 1, 1))
 
         for d in ALL:
             cp_att(j, d).start()
@@ -467,19 +502,20 @@
     stage_a(1)
 
     def step(j, _):
-        stage_c(j)
-
-        @pl.when(j + 3 < STEPS)
-        def _():
-            front(j + 3)
-
-        @pl.when(j + 1 < STEPS)
-        def _():
-            stage_b(j + 1)
-
-        @pl.when(j + 2 < STEPS)
-        def _():
-            stage_a(j + 2)
+        def between(v):
+            @pl.when((v == 0) & (j + 1 < STEPS))
+            def _():
+                stage_b(j + 1)
+
+            @pl.when((v == 1) & (j + 2 < STEPS))
+            def _():
+                stage_a(j + 2)
+
+            @pl.when((v == 1) & (j + 3 < STEPS))
+            def _():
+                front(j + 3)
+
+        stage_c(j, between)
 
         @pl.when(j >= 1)
         def _():
@@ -571,20 +607,19 @@
     first = jnp.arange(blocks, dtype=jnp.int32)[:, None]
     col = jnp.arange(BLK, dtype=jnp.int32)[None, :]
     offset = col - first
-    onehot = offset[:, :, None] == jnp.arange(span_, dtype=jnp.int32)[None, None, :]
-    picked = jnp.sum(jnp.where(onehot, rows[:, None, :], 0), axis=-1)
+    picked = sum(jnp.where(offset == k, rows[:, k : k + 1], 0) for k in range(span_))
     globe = x * blocks - reach + col
     inside = (globe >= 0) & (globe < pattern.shape[0])
     allowed = ((picked > 0) & inside) | (col >= EXT // BLK)
-    return jnp.repeat(jnp.where(allowed, 0.0, NEG).astype(bf16), BLK, axis=0)
+    return jnp.where(allowed, 0.0, NEG).astype(f32)
 
 
 def local(hidden, query_norm_gain, key_norm_gain, text_kv, holder, pattern, grad_out):
     x = lax.axis_index("seq") // NY
     qbias = query_bias(pattern, x)
     who = holder[0]
-    select = jnp.concatenate([jnp.arange(NX) == who // NY, jnp.arange(NY) == who % NY])
-    select = jnp.broadcast_to(select.astype(f32)[:, None], (NX + NY, NY * BLK))
+    row = lax.broadcasted_iota(jnp.int32, (NX + NY, NY * BLK), 0)
+    select = jnp.where(row < NX, row == who // NY, row - NX == who % NY).astype(f32)
     heads = WIDTH // HDIM
     any_spec = pl.BlockSpec(memory_space=pl.ANY)
     vmem = pl.BlockSpec(memory_space=pltpu.VMEM)
@@ -618,8 +653,14 @@
             V(BLK, KEYS),
             V(BLK + 16, KEYS),
             V(QT, 2 * BLK),
+            V(QT, 2 * BLK),
             V(NCHUNK, KC, QT, dtype=f32),
             V(NCHUNK, KC, QT),
+            V(NCHUNK, KC, QT),
+            V(BLK, QT),
+            V(BLK, QT),
+            V(8, QT, dtype=f32),
+            V(8, QT, dtype=f32),
             V(KEYS, BLK, dtype=f32),
             V(KEYS, BLK, dtype=f32),
             V(OWN, BLK, dtype=f32),

time: 221 us -> 185 us (0.84)
  Pallas kernels: 206 us -> 170 us
    pallas_call x1, Pallas kernels: 206 us -> 170 us  [local(): pl.pallas_call(kernel, out_shape=(jax.ShapeDtypeStruct((SLAB, WIDTH), bf1...]
where the time goes in v3:
time: 185 us; the launch traced here: 184 us
  Pallas kernels  170 us (92%)
  local copies, waits for them, and re-layouts  9.16 us (5%)
  other arithmetic  3.36 us (2%)
    pallas_call x1, Pallas kernels, local(): pl.pallas_call(kernel, out_shape=(jax.ShapeDtypeStruct((SLAB, WIDTH), bf1...  170 us
    unnamed x7, local copies, waits for them, and re-layouts  8.41 us

profile of v3, /device:TPU:1, one launch (start us, length us, event | category | flops | bytes accessed | tf_op | source)
XLA Modules:
  0.0 183.6 jit_solution(8667693791067263188)
XLA Ops:
  0.6 0.0 copy-start
  1.4 0.0 copy-done
  1.4 0.1 constant_dynamic-slice_fusion
  1.5 0.7 fusion.9.qb_ref
  2.1 1.3 reduce
  3.5 1.3 reduce.1
  4.8 0.7 iota.27.sel_ref
  5.5 169.7 %attention.1 = (bf16[384,2560]{1,0:T(8,128)(2,1)}, bf16[384,2560]{1,0:T(8,128)(2,1)}, bf16[2,512,2560]{2,1,0:T(8,128)(2,1)}) custom-call(bf16[384,2560]{1,0:T(8,128)(2,1)} %bitcast.33, bf16[384,2560]{1,0:T(8,128)(2,1)} %bitcast.34, bf16[2,512,2560]{2,1,0:T(8,128)(2,1)} %bitcast.32, f32[20,128]{1,0:T(8,128)} %bitcast.30, f32[20,128]{1,0:T(8,128)} %bitcast.31, ...), custom_call_target="tpu_custom_call" | custom-call | flops 24000000000 | bytes 40000000 | tf_op jit(solution)/shard_map/attention/pallas_call | solution.py:630
  175.2 0.0 copy-start.1
  175.2 3.1 %copy.14 = bf16[1,384,2560]{2,1,0:T(8,128)(2,1)} copy(bf16[1,384,2560]{2,1,0:T(8,128)(2,1)} %bitcast.29) | data formatting | bytes 3932160
  178.3 2.9 %copy.15 = bf16[1,384,2560]{2,1,0:T(8,128)(2,1)} copy(bf16[1,384,2560]{2,1,0:T(8,128)(2,1)} %bitcast.28) | data formatting | bytes 3932160
  181.3 0.0 copy-done.1
  181.3 2.4 %copy.16 = bf16[1,2,512,2560]{3,2,1,0:T(8,128)(2,1)} copy(bf16[1,2,512,2560]{3,2,1,0:T(8,128)(2,1)S(1)} %bitcast.27) | data formatting | bytes 10485760
  (3 shorter events, 0.0 us)
Async XLA Ops:
  0.6 0.7 copy-start
  175.2 6.0 %copy-start.1 = (bf16[2,512,2560]{2,1,0:T(8,128)(2,1)S(1)}, bf16[2,512,2560]{2,1,0:T(8,128)(2,1)}, u32[]{:S(2)}) copy-start(bf16[2,512,2560]{2,1,0:T(8,128)(2,1)} %get-tuple-element.8) | copy-start | bytes 15728644

commit v4 on v3

--- a/solution.py
+++ b/solution.py
@@ -39,8 +39,9 @@
     K_RS,
     K_G1,
     K_G2,
-) = range(12)
-KINDS = 12
+    K_G3,
+) = range(13)
+KINDS = 13
 O_R, O_RH, O_MH, O_M, O_HU = range(5)
 
 f32 = jnp.float32
@@ -84,7 +85,7 @@
 def kernel(
     hid, do_in, txt, gq_ref, gk_ref, sel_ref, qb_ref,
     att_out, dh_out, tg_out,
-    HS, HU, RU, HX, DO, RTX, RT, RB, T1, TS, T2, T3, KA, KT, VT, QA0, QA1, S, PB0, PB1, DTS0, DTS1, DL0, DL1, DK, DV, DQ,
+    HS, HU, RU, HX, DO, RTX, RT, RB, TP, TQ, TM, T1, TS, T2, T3, KA, KT, VT, QA0, QA1, S, PB0, PB1, DTS0, DTS1, DL0, DL1, DK, DV, DQ,
     ATT, AFS, AH, AHR, AO, AF, M, MH, MT, MHS, MHR, MR, TGP, TG1, TG2, TGY, TGX, DH,
     send, recv, once_send, once_recv, loc, loc1,
 ):
@@ -143,8 +144,17 @@
     def cp_do(j, d, w=False):
         return rc(do_in.at[:, hcol(j, ry(d))], DO.at[j, oslab(ry(-d) if w else y), :], K_DO, j, d, yid(d))
 
-    def cp_tx(j, d, w=False):
-        return rc(txt.at[:, block(rx(d)), wide(j)], T1.at[j, rx(-d) if w else x], K_TX, j, d, xid(d))
+    def cp_tx_far(j, d, w=False):
+        kv = 0 if d == 1 else 1
+        return rc(txt.at[kv, block(rx(2)), wide(j)], TP.at[j, kv], K_TX, j, d, xid(d))
+
+    def cp_tx_near(j, d, w=False):
+        side, kv = (0, 1) if d == 1 else (1, 0)
+        return rc(txt.at[kv, block(rx(d)), wide(j)], T1.at[j, side, kv], K_TX, j, 4 + d, xid(d))
+
+    def cp_tx_pass(j, d, w=False):
+        kv = 0 if d == 1 else 1
+        return rc(TM.at[j, kv], T1.at[j, kv, kv], K_TX, j, 1 + d, xid(d))
 
     def cp_ty(j, d, w=False):
         return rc(TS.at[j, :, :, block(ry(d))], T2.at[j, ry(-d) if w else y], K_TY, j, d, yid(d))
@@ -182,6 +192,19 @@
     def cp_g2v(j, d, w=False):
         return rc(TGX.at[j], tg_out.at[1, :, hcol(j, ry(-d) if w else y)], K_G2, j, 4 + d, yid(d))
 
+    def cp_g3k(j, d, w=False):
+        part = 0 if d == 1 else 1
+        who = rx(2) if w else rx(-d)
+        half = BLK // 2
+        rows = span(who * BLK + part * half, half, half)
+        return rc(tg_out.at[0, rows, wide(j)], tg_out.at[0, rows, wide(j)], K_G3, j, d, xid(d))
+
+    def cp_g3v(j, d, w=False):
+        part = 0 if d == 1 else 1
+        who = ry(2) if w else ry(-d)
+        rows = pl.ds(part * (TXT // 2), TXT // 2)
+        return rc(tg_out.at[1, rows, hcol(j, who)], tg_out.at[1, rows, hcol(j, who)], K_G3, j, 4 + d, yid(d))
+
     def cp_r(d, w=False):
         return rc1(RT, RTX.at[span(24 + 24 * (ry(-d) if w else y), 24, 8), :], O_R, d, yid(d))
 
@@ -210,7 +233,11 @@
         return pltpu.make_async_copy(do_in.at[:, hcol(j, y)], DO.at[j, oslab(y), :], loc.at[1, j])
 
     def lo_tx(j):
-        return pltpu.make_async_copy(txt.at[:, block(x), wide(j)], T1.at[j, x], loc.at[2, j])
+        return pltpu.make_async_copy(txt.at[:, block(x), wide(j)], T1.at[j, 2], loc.at[2, j])
+
+    def lo_pass(j, kv):
+        where = rx(1) if kv == 0 else rx(-1)
+        return pltpu.make_async_copy(txt.at[kv, block(where), wide(j)], TQ.at[j, kv], loc.at[6 + kv, j])
 
     def lo_att(j):
         return pltpu.make_async_copy(ATT.at[j, oslab(y), :], att_out.at[:, hcol(j, y)], loc.at[3, j])
@@ -226,20 +253,35 @@
     SIDES = (1, 3)
 
     def front(j):
-        for d in ALL:
-            cp_tx(j, d).start()
+        for d in SIDES:
+            cp_tx_far(j, d).start()
+        for d in SIDES:
+            cp_tx_near(j, d).start()
+        for d in ALL:
             cp_h(j, d).start()
         for d in ALL:
             cp_do(j, d).start()
+
+    def stage_p(j):
+        for kv in range(2):
+            lo_pass(j, kv).wait()
+            cp_tx_far(j, 1 if kv == 0 else 3, True).wait_recv()
+            far = sel_ref[3:4, :] if kv == 0 else sel_ref[1:2, :]
+            part = TP[j, kv].astype(f32) * far + TQ[j, kv].astype(f32) * (1.0 - far)
+            TM[j, kv] = part.astype(bf16)
+            cp_tx_pass(j, 1 if kv == 0 else 3).start()
 
     def stage_a(j):
         lo_tx(j).wait()
-        for d in ALL:
-            cp_tx(j, d, True).wait_recv()
+        for d in SIDES:
+            cp_tx_near(j, d, True).wait_recv()
+            cp_tx_pass(j, d, True).wait_recv()
+        here, up, two, down = (sel_ref[k : k + 1, :] for k in range(NX))
         for kv in range(2):
-            part = jnp.zeros((BLK, NY * BLK), f32)
-            for k in range(NX):
-                part = part + T1[j, k, kv].astype(f32) * sel_ref[k : k + 1, :]
+            low, high = (down + two, up) if kv == 0 else (down, up + two)
+            part = T1[j, 2, kv].astype(f32) * here
+            part = part + T1[j, 0, kv].astype(f32) * low
+            part = part + T1[j, 1, kv].astype(f32) * high
             TS[j, kv] = part.astype(bf16)
         T2[j, y] = TS[j, :, :, block(y)]
         for d in ALL:
@@ -432,11 +474,18 @@
         for d in ALL:
             cp_g1k(j, d, True).wait_recv()
             cp_g1v(j, d, True).wait_recv()
-        for d in ALL:
+        for d in SIDES:
             cp_g2k(j, d).start()
             cp_g2v(j, d).start()
         lo_g2k(j).start()
         lo_g2v(j).start()
+
+    def stage_f(j):
+        for d in SIDES:
+            cp_g2k(j, d, True).wait_recv()
+            cp_g3k(j, d).start()
+            cp_g2v(j, d, True).wait_recv()
+            cp_g3v(j, d).start()
 
     barrier = pltpu.get_barrier_semaphore()
     for d in ALL:
@@ -450,6 +499,8 @@
     def first_local(j, _):
         lo_h(j).start()
         lo_tx(j).start()
+        lo_pass(j, 0).start()
+        lo_pass(j, 1).start()
         lo_do(j).start()
         return 0
 
@@ -458,6 +509,7 @@
 
     front(0)
     cp_hu().start()
+    stage_p(0)
 
     lane = lax.broadcasted_iota(jnp.int32, (BLK, BLK), 1)
 
@@ -498,6 +550,7 @@
     for b in range(EXT // BLK):
         RB[b * BLK : (b + 1) * BLK, :] = unpacked(RTX[8 * b : 8 * b + 8, :])
     stage_b(0)
+    stage_p(1)
     front(2)
     stage_a(1)
 
@@ -507,6 +560,10 @@
             def _():
                 stage_b(j + 1)
 
+            @pl.when((v == 0) & (j + 2 < STEPS))
+            def _():
+                stage_p(j + 2)
+
             @pl.when((v == 1) & (j + 2 < STEPS))
             def _():
                 stage_a(j + 2)
@@ -524,6 +581,10 @@
         @pl.when(j >= 2)
         def _():
             stage_e(j - 2)
+
+        @pl.when(j >= 3)
+        def _():
+            stage_f(j - 3)
 
         return 0
 
@@ -535,17 +596,20 @@
             MHS[k, 8 * b : 8 * b + 8, :] = tiles[b]
     for d in SIDES:
         cp_mh(d).start()
+    stage_d(STEPS - 1)
+    stage_e(STEPS - 2)
     for b in range(OWN // BLK):
         column = jnp.sum(M[b * BLK : (b + 1) * BLK, :], axis=1, keepdims=True)
         MT[8 * b : 8 * b + 8, :] = packed(column)[0]
-    stage_d(STEPS - 1)
     for d in SIDES:
         cp_mh(d, True).wait_recv()
     MT[:24, :] += MHR[0]
     MT[72:96, :] += MHR[1]
     for d in FOUR:
         cp_m(d).start()
-    stage_e(STEPS - 2)
+    stage_e(STEPS - 1)
+    stage_f(STEPS - 3)
+    stage_f(STEPS - 2)
     cp_hu().wait_recv()
     cp_ru().wait_recv()
     for d in FOUR:
@@ -567,19 +631,24 @@
         DH[rows, :] = jnp.where(section < sections - 1, grad, 0.0).astype(bf16)
     store = pltpu.make_async_copy(DH, dh_out, loc1.at[1])
     store.start()
-    stage_e(STEPS - 1)
+    stage_f(STEPS - 1)
     store.wait()
 
     def last(j, _):
         for d in ALL:
             cp_att(j, d, True).wait_recv()
-            cp_g2k(j, d, True).wait_recv()
-            cp_g2v(j, d, True).wait_recv()
-            for copy in (cp_h, cp_do, cp_tx, cp_ty, cp_tg, cp_att, cp_rs, cp_g1k, cp_g1v, cp_g2k, cp_g2v):
+            for copy in (cp_h, cp_do, cp_ty, cp_tg, cp_att, cp_rs, cp_g1k, cp_g1v):
                 copy(j, d).wait_send()
         for d in FOUR:
             cp_a(j, d).wait_send()
         for d in SIDES:
+            cp_g3k(j, d, True).wait_recv()
+            cp_g3v(j, d, True).wait_recv()
+            for copy in (cp_g2k, cp_g2v, cp_g3k, cp_g3v):
+                copy(j, d).wait_send()
+            cp_tx_far(j, d).wait_send()
+            cp_tx_near(j, d).wait_send()
+            cp_tx_pass(j, d).wait_send()
             cp_halo(j, d).wait_send()
             cp_ah(j, d).wait_send()
         lo_att(j).wait()
@@ -619,7 +688,7 @@
     qbias = query_bias(pattern, x)
     who = holder[0]
     row = lax.broadcasted_iota(jnp.int32, (NX + NY, NY * BLK), 0)
-    select = jnp.where(row < NX, row == who // NY, row - NX == who % NY).astype(f32)
+    select = jnp.where(row < NX, row == (who // NY - x + NX) % NX, row - NX == who % NY).astype(f32)
     heads = WIDTH // HDIM
     any_spec = pl.BlockSpec(memory_space=pl.ANY)
     vmem = pl.BlockSpec(memory_space=pltpu.VMEM)
@@ -645,7 +714,10 @@
             V(EXT // BLK * 8, BLK, dtype=f32),
             V(24, BLK, dtype=f32),
             V(EXT, BLK, dtype=f32),
-            V(STEPS, NX, 2, BLK, NY * BLK),
+            V(STEPS, 2, BLK, NY * BLK),
+            V(STEPS, 2, BLK, NY * BLK),
+            V(STEPS, 2, BLK, NY * BLK),
+            V(STEPS, 3, 2, BLK, NY * BLK),
             V(STEPS, 2, BLK, NY * BLK),
             V(STEPS, NY, 2, BLK, BLK),
             V(STEPS, 2, TXT, BLK),
@@ -686,7 +758,7 @@
             pltpu.SemaphoreType.DMA((KINDS, STEPS, 8)),
             pltpu.SemaphoreType.DMA((5, 4)),
             pltpu.SemaphoreType.DMA((5, 4)),
-            pltpu.SemaphoreType.DMA((6, STEPS)),
+            pltpu.SemaphoreType.DMA((8, STEPS)),
             pltpu.SemaphoreType.DMA((2,)),
         ],
         compiler_params=pltpu.CompilerParams(

time: 185 us -> 176 us (0.951)
  Pallas kernels: 170 us -> 162 us
    pallas_call x1, Pallas kernels: 170 us -> 162 us  [local(): pl.pallas_call(kernel, out_shape=(jax.ShapeDtypeStruct((SLAB, WIDTH), bf1...]
where the time goes in v4:
time: 176 us
  Pallas kernels  162 us (92%)
  local copies, waits for them, and re-layouts  9.16 us (5%)
  other arithmetic  3.36 us (2%)
    pallas_call x1, Pallas kernels, local(): pl.pallas_call(kernel, out_shape=(jax.ShapeDtypeStruct((SLAB, WIDTH), bf1...  162 us
    unnamed x7, local copies, waits for them, and re-layouts  8.41 us

profile of v4, /device:TPU:1, one launch (start us, length us, event | category | flops | bytes accessed | tf_op | source)
XLA Modules:
  0.0 176.1 jit_solution(14280881468030163685)
XLA Ops:
  0.6 0.0 copy-start
  1.4 0.0 copy-done
  1.4 0.1 constant_dynamic-slice_fusion
  1.5 0.7 fusion.9.qb_ref
  2.2 1.3 reduce
  3.5 1.3 reduce.1
  4.8 0.7 iota.27.sel_ref
  5.5 162.2 %attention.1 = (bf16[384,2560]{1,0:T(8,128)(2,1)}, bf16[384,2560]{1,0:T(8,128)(2,1)}, bf16[2,512,2560]{2,1,0:T(8,128)(2,1)}) custom-call(bf16[384,2560]{1,0:T(8,128)(2,1)} %bitcast.33, bf16[384,2560]{1,0:T(8,128)(2,1)} %bitcast.34, bf16[2,512,2560]{2,1,0:T(8,128)(2,1)} %bitcast.32, f32[20,128]{1,0:T(8,128)} %bitcast.30, f32[20,128]{1,0:T(8,128)} %bitcast.31, ...), custom_call_target="tpu_custom_call" | custom-call | flops 24000000000 | bytes 40000000 | tf_op jit(solution)/shard_map/attention/pallas_call | solution.py:699
  167.7 0.0 copy-start.1
  167.8 3.1 %copy.14 = bf16[1,384,2560]{2,1,0:T(8,128)(2,1)} copy(bf16[1,384,2560]{2,1,0:T(8,128)(2,1)} %bitcast.29) | data formatting | bytes 3932160
  170.8 2.9 %copy.15 = bf16[1,384,2560]{2,1,0:T(8,128)(2,1)} copy(bf16[1,384,2560]{2,1,0:T(8,128)(2,1)} %bitcast.28) | data formatting | bytes 3932160
  173.8 0.0 copy-done.1
  173.8 2.4 %copy.16 = bf16[1,2,512,2560]{3,2,1,0:T(8,128)(2,1)} copy(bf16[1,2,512,2560]{3,2,1,0:T(8,128)(2,1)S(1)} %bitcast.27) | data formatting | bytes 10485760
  (3 shorter events, 0.0 us)
Async XLA Ops:
  0.6 0.8 copy-start
  167.7 6.0 %copy-start.1 = (bf16[2,512,2560]{2,1,0:T(8,128)(2,1)S(1)}, bf16[2,512,2560]{2,1,0:T(8,128)(2,1)}, u32[]{:S(2)}) copy-start(bf16[2,512,2560]{2,1,0:T(8,128)(2,1)} %get-tuple-element.8) | copy-start | bytes 15728644

commit v5 on v4

--- a/solution.py
+++ b/solution.py
@@ -310,9 +310,8 @@
         for d in ALL:
             cp_do(j, d, True).wait_recv()
             cp_tg(j, d, True).wait_recv()
-        head = NY * j + y
-        gq = gq_ref[pl.ds(head, 1), :]
-        gk = gk_ref[pl.ds(head, 1), :]
+        gq = gq_ref[:, hcol(j, y)]
+        gk = gk_ref[:, hcol(j, y)]
         par = lax.rem(j, 2)
 
         def prep(b, _):
@@ -553,6 +552,7 @@
     stage_p(1)
     front(2)
     stage_a(1)
+    front(3)
 
     def step(j, _):
         def between(v):
@@ -568,9 +568,9 @@
             def _():
                 stage_a(j + 2)
 
-            @pl.when((v == 1) & (j + 3 < STEPS))
+            @pl.when((v == 1) & (j + 4 < STEPS))
             def _():
-                front(j + 3)
+                front(j + 4)
 
         stage_c(j, between)
 
@@ -689,7 +689,6 @@
     who = holder[0]
     row = lax.broadcasted_iota(jnp.int32, (NX + NY, NY * BLK), 0)
     select = jnp.where(row < NX, row == (who // NY - x + NX) % NX, row - NX == who % NY).astype(f32)
-    heads = WIDTH // HDIM
     any_spec = pl.BlockSpec(memory_space=pl.ANY)
     vmem = pl.BlockSpec(memory_space=pltpu.VMEM)
 
@@ -772,8 +771,8 @@
         hidden[0],
         grad_out[0],
         text_kv[0, 0],
-        query_norm_gain.reshape(heads, HDIM),
-        key_norm_gain.reshape(heads, HDIM),
+        query_norm_gain,
+        key_norm_gain,
         select,
         qbias,
     )

time: 176 us -> 173 us (0.983)
  other arithmetic: 3.36 us -> 0.71 us
    unnamed x2 -> x0, other arithmetic: 2.66 us -> none
where the time goes in v5:
time: 173 us; the launch traced here: 172 us
  Pallas kernels  161 us (93%)
  local copies, waits for them, and re-layouts  9.16 us (5%)
    pallas_call x1, Pallas kernels, local(): pl.pallas_call(kernel, out_shape=(jax.ShapeDtypeStruct((SLAB, WIDTH), bf1...  161 us
    unnamed x7, local copies, waits for them, and re-layouts  8.41 us

profile of v5, /device:TPU:1, one launch (start us, length us, event | category | flops | bytes accessed | tf_op | source)
XLA Modules:
  0.0 172.4 jit_solution(9210122578784273321)
XLA Ops:
  0.6 0.0 copy-start
  1.4 0.0 copy-done
  1.4 0.1 constant_dynamic-slice_fusion
  1.5 0.7 fusion.9.qb_ref
  2.2 0.7 iota.27.sel_ref
  2.8 161.2 %attention.1 = (bf16[384,2560]{1,0:T(8,128)(2,1)}, bf16[384,2560]{1,0:T(8,128)(2,1)}, bf16[2,512,2560]{2,1,0:T(8,128)(2,1)}) custom-call(bf16[384,2560]{1,0:T(8,128)(2,1)} %bitcast.29, bf16[384,2560]{1,0:T(8,128)(2,1)} %bitcast.30, bf16[2,512,2560]{2,1,0:T(8,128)(2,1)} %bitcast.28, f32[1,2560]{1,0:T(1,128)} %gq_ref.1, f32[1,2560]{1,0:T(1,128)} %gk_ref.1, ...), custom_call_target="tpu_custom_call" | custom-call | flops 24000000000 | bytes 40000000 | tf_op jit(solution)/shard_map/attention/pallas_call | solution.py:698
  164.0 0.0 copy-start.1
  164.0 3.1 %copy.14 = bf16[1,384,2560]{2,1,0:T(8,128)(2,1)} copy(bf16[1,384,2560]{2,1,0:T(8,128)(2,1)} %bitcast.27) | data formatting | bytes 3932160
  167.1 2.9 %copy.15 = bf16[1,384,2560]{2,1,0:T(8,128)(2,1)} copy(bf16[1,384,2560]{2,1,0:T(8,128)(2,1)} %bitcast.26) | data formatting | bytes 3932160
  170.1 0.0 copy-done.1
  170.1 2.4 %copy.16 = bf16[1,2,512,2560]{3,2,1,0:T(8,128)(2,1)} copy(bf16[1,2,512,2560]{3,2,1,0:T(8,128)(2,1)S(1)} %bitcast.25) | data formatting | bytes 10485760
  (3 shorter events, 0.0 us)
Async XLA Ops:
  0.6 0.8 copy-start
  164.0 6.0 %copy-start.1 = (bf16[2,512,2560]{2,1,0:T(8,128)(2,1)S(1)}, bf16[2,512,2560]{2,1,0:T(8,128)(2,1)}, u32[]{:S(2)}) copy-start(bf16[2,512,2560]{2,1,0:T(8,128)(2,1)} %get-tuple-element.8) | copy-start | bytes 15728644

commit v6 on v5

--- a/solution.py
+++ b/solution.py
@@ -302,6 +302,11 @@
             T3[j, kv, block(x), :] = part.astype(bf16)
         for d in ALL:
             cp_tg(j, d).start()
+
+    def send_att(j):
+        for d in ALL:
+            cp_att(j, d).start()
+        lo_att(j).start()
 
     def stage_c(j, between):
         for d in SIDES:
@@ -413,9 +418,9 @@
         woven(forward(tiles - 1, 1), backward(tiles - 2, 0))
         woven(backward(tiles - 1, 1))
 
-        for d in ALL:
-            cp_att(j, d).start()
-        lo_att(j).start()
+        @pl.when(j < STEPS - 1)
+        def _():
+            send_att(j)
 
         for k in range(2):
             rows = slice(k * (OWN + SLAB), k * (OWN + SLAB) + SLAB)
@@ -597,6 +602,7 @@
     for d in SIDES:
         cp_mh(d).start()
     stage_d(STEPS - 1)
+    send_att(STEPS - 1)
     stage_e(STEPS - 2)
     for b in range(OWN // BLK):
         column = jnp.sum(M[b * BLK : (b + 1) * BLK, :], axis=1, keepdims=True)

time: 173 us -> 173 us (level)
  no operation moved by 1% of the time
where the time goes in v6:
time: 173 us
  Pallas kernels  161 us (93%)
  local copies, waits for them, and re-layouts  9.16 us (5%)
    pallas_call x1, Pallas kernels, local(): pl.pallas_call(kernel, out_shape=(jax.ShapeDtypeStruct((SLAB, WIDTH), bf1...  161 us
    unnamed x7, local copies, waits for them, and re-layouts  8.41 us

profile of v6, /device:TPU:1, one launch (start us, length us, event | category | flops | bytes accessed | tf_op | source)
XLA Modules:
  0.0 172.6 jit_solution(2118109877405217961)
XLA Ops:
  0.6 0.0 copy-start
  1.4 0.0 copy-done
  1.4 0.1 constant_dynamic-slice_fusion
  1.5 0.7 fusion.9.qb_ref
  2.2 0.7 iota.27.sel_ref
  2.8 161.3 %attention.1 = (bf16[384,2560]{1,0:T(8,128)(2,1)}, bf16[384,2560]{1,0:T(8,128)(2,1)}, bf16[2,512,2560]{2,1,0:T(8,128)(2,1)}) custom-call(bf16[384,2560]{1,0:T(8,128)(2,1)} %bitcast.29, bf16[384,2560]{1,0:T(8,128)(2,1)} %bitcast.30, bf16[2,512,2560]{2,1,0:T(8,128)(2,1)} %bitcast.28, f32[1,2560]{1,0:T(1,128)} %gq_ref.1, f32[1,2560]{1,0:T(1,128)} %gk_ref.1, ...), custom_call_target="tpu_custom_call" | custom-call | flops 24000000000 | bytes 40000000 | tf_op jit(solution)/shard_map/attention/pallas_call | solution.py:704
  164.2 0.0 copy-start.1
  164.2 3.1 %copy.14 = bf16[1,384,2560]{2,1,0:T(8,128)(2,1)} copy(bf16[1,384,2560]{2,1,0:T(8,128)(2,1)} %bitcast.27) | data formatting | bytes 3932160
  167.3 2.9 %copy.15 = bf16[1,384,2560]{2,1,0:T(8,128)(2,1)} copy(bf16[1,384,2560]{2,1,0:T(8,128)(2,1)} %bitcast.26) | data formatting | bytes 3932160
  170.2 0.0 copy-done.1
  170.2 2.4 %copy.16 = bf16[1,2,512,2560]{3,2,1,0:T(8,128)(2,1)} copy(bf16[1,2,512,2560]{3,2,1,0:T(8,128)(2,1)S(1)} %bitcast.25) | data formatting | bytes 10485760
  (3 shorter events, 0.0 us)
Async XLA Ops:
  0.6 0.8 copy-start
  164.2 6.0 %copy-start.1 = (bf16[2,512,2560]{2,1,0:T(8,128)(2,1)S(1)}, bf16[2,512,2560]{2,1,0:T(8,128)(2,1)}, u32[]{:S(2)}) copy-start(bf16[2,512,2560]{2,1,0:T(8,128)(2,1)} %get-tuple-element.8) | copy-start | bytes 15728644
